TPU v7x, 256 devices: a whole 4x4x8 slice. The times are simulated.
256 devices in a mesh: tile: 32 (over x, y, z_lo), frame: 8 (over z_hi, core).
Axes of the slice: x: 4, y: 4, z: 8 (z_hi: 4, z_lo: 2; z = z_hi * 2 + z_lo), core: 2. Of those that a mesh axis runs over, the one named last changes fastest.
Arguments:
- latents: bfloat16 [128, 8, 104, 384], P('tile', 'frame'), may hold values from -80 to 80
- row_video: int32 [128], replicated, may hold values from 0 to 3, never falling along the last dimension, each value on 1 to 90 neighbouring positions
- video_cols: int32 [4], replicated, may hold values from 52 to 104, as said below
- first_gain: float32 [384], replicated, may hold values from 0.5 to 1.5
- first_shift: float32 [384], replicated, may hold values from -3 to 3
- conv_weight: bfloat16 [3, 3, 3, 384, 384], replicated, may hold values from -0.0625 to 0.0625
- conv_bias: float32 [384], replicated, may hold values from -3 to 3
- second_gain: float32 [384], replicated, may hold values from 0.5 to 1.5
- second_shift: float32 [384], replicated, may hold values from -3 to 3
- triple_weight: bfloat16 [384, 1152], replicated, may hold values from -0.55 to 0.55
- triple_bias: float32 [1152], replicated, may hold values from -3 to 3
- output_weight: bfloat16 [384, 384], replicated, may hold values from -0.3125 to 0.3125
- output_bias: float32 [384], replicated, may hold values from -3 to 3
- upsample_weight: bfloat16 [3, 3, 384, 192], replicated, may hold values from -0.109375 to 0.109375
- upsample_bias: float32 [192], replicated, may hold values from -3 to 3
Outputs:
- decoded: bfloat16 [256, 8, 208, 192], P('tile', 'frame')
Inputs may be any that keep to these rules, and one draw needn't show every extreme that they name: `row_video`: video numbers never fall along the rows; every video has 1 to 90 rows. `video_cols`: one video has all 104 columns.
All inputs are finite; a program needn't handle non-finite values.
Results may differ from a plain program's by a relative error of at most 0.013.
The roundings to bfloat16 on the way count: a program that leaves them out, or rounds other values in their place, can miss the bound.
Values may be sent and summed in bfloat16 or wider, within the bound.
A program may use at most 128 MiB of HBM per device.

v0:
```python
import jax
import jax.numpy as jnp
from jax import lax
from jax.sharding import PartitionSpec as P

GROUPS = 32


EPSILON = 1e-05
MASKED = -1e30
HIGHEST = lax.Precision.HIGHEST


def shifted(shard, axis, by):
    length = lax.axis_size(axis)
    pairs = [(i, i + by) for i in range(length) if 0 <= i + by < length]
    return lax.ppermute(shard, axis, pairs)


def padded_2(shard, sides, width):
    for axis, dim in sides:
        size, length = (lax.axis_size(axis), shard.shape[dim])
        up = [(i, (i + 1) % size) for i in range(size - 1)]
        down = [(j, i) for i, j in up]
        last = lax.slice_in_dim(shard, length - width, length, axis=dim)
        leading = lax.slice_in_dim(shard, 0, width, axis=dim)
        before = lax.ppermute(last, axis, up)
        after = lax.ppermute(leading, axis, down)
        shard = jnp.concatenate([before, shard, after], axis=dim)
    return shard


def video_lookup(labels, video_cols):
    numbers = jnp.arange(video_cols.shape[0], dtype=jnp.int32)
    matches = labels[:, None] == numbers[None, :]
    widths = jnp.sum(jnp.where(matches, video_cols[None, :], 0), axis=1)
    return (matches.astype(jnp.float32), widths)


def group_norm(values, norm_gain, norm_shift, onehot, valid_mask, counts):
    channels = values.shape[3]
    per_group = channels // GROUPS
    member = (
        jnp.arange(channels, dtype=jnp.int32)[:, None] // per_group
        == jnp.arange(GROUPS, dtype=jnp.int32)[None, :]
    ).astype(jnp.float32)
    mask_four = valid_mask.astype(jnp.float32)[:, None, :, None]
    masked = values * mask_four
    partial_sum = jnp.einsum("rfwc,cg,rv->fvg", masked, member, onehot, precision=HIGHEST)
    group_mean = lax.psum(partial_sum, "tile") / counts
    mean_full = jnp.einsum("fvg,rv,cg->rfc", group_mean, onehot, member, precision=HIGHEST)
    centered = (values - mean_full[:, :, None, :]) * mask_four
    partial_spread = jnp.einsum(
        "rfwc,cg,rv->fvg", centered * centered, member, onehot, precision=HIGHEST
    )
    variance = lax.psum(partial_spread, "tile") / counts
    scale_full = jnp.einsum(
        "fvg,rv,cg->rfc", lax.rsqrt(variance + EPSILON), onehot, member, precision=HIGHEST
    )
    return centered * scale_full[:, :, None, :] * norm_gain + norm_shift


def causal_context(hidden):
    earlier = shifted(hidden, "frame", 1)
    farther = shifted(hidden, "frame", 2)
    earlier = jnp.concatenate([farther, earlier], axis=1)
    stacked = jnp.concatenate([earlier, hidden], axis=1)
    context = padded_2(stacked, (("tile", 0),), 1)
    return context


def conv_taps(context, conv_weight, near_labels, own_labels):
    row_count = own_labels.shape[0]
    frame_count = context.shape[1] - 2
    col_count = context.shape[2]
    channels = context.shape[3]
    padded = jnp.pad(context, ((0, 0), (0, 0), (1, 1), (0, 0)))
    total = jnp.zeros((row_count * frame_count * col_count, conv_weight.shape[-1]), jnp.float32)
    for row_tap in range(3):
        same = (near_labels[row_tap : row_tap + row_count] == own_labels).astype(context.dtype)[
            :, None, None, None
        ]
        for time_tap in range(3):
            window = padded[row_tap : row_tap + row_count, time_tap : time_tap + frame_count] * same
            columns = jnp.concatenate(
                [window[:, :, col_tap : col_tap + col_count] for col_tap in range(3)], axis=-1
            )
            total = total + jnp.dot(
                columns.reshape(-1, 3 * channels),
                conv_weight[time_tap, row_tap].reshape(3 * channels, -1),
                preferred_element_type=jnp.float32,
            )
    return total.reshape(row_count, frame_count, col_count, -1)


def upsample_conv(rimmed, weight, near_labels, own_labels):
    row_count = own_labels.shape[0]
    frame_count = rimmed.shape[1]
    wide_count = 2 * rimmed.shape[2]
    channels = rimmed.shape[3]
    doubled = jnp.repeat(jnp.repeat(rimmed, 2, axis=0), 2, axis=2)[1 : 2 * row_count + 3]
    doubled = jnp.pad(doubled, ((0, 0), (0, 0), (1, 1), (0, 0)))
    up_labels = jnp.repeat(near_labels, 2)[1 : 2 * row_count + 3]
    target_labels = jnp.repeat(own_labels, 2)
    total = jnp.zeros((2 * row_count * frame_count * wide_count, weight.shape[-1]), jnp.float32)
    for row_tap in range(3):
        same = (up_labels[row_tap : row_tap + 2 * row_count] == target_labels).astype(rimmed.dtype)[
            :, None, None, None
        ]
        window = doubled[row_tap : row_tap + 2 * row_count] * same
        columns = jnp.concatenate(
            [window[:, :, col_tap : col_tap + wide_count] for col_tap in range(3)], axis=-1
        )
        total = total + jnp.dot(
            columns.reshape(-1, 3 * channels),
            weight[row_tap].reshape(3 * channels, -1),
            preferred_element_type=jnp.float32,
        )
    return total.reshape(2 * row_count, frame_count, wide_count, -1)


def shards(
    latents,
    row_video,
    video_cols,
    first_gain,
    first_shift,
    conv_weight,
    conv_bias,
    second_gain,
    second_shift,
    triple_weight,
    triple_bias,
    output_weight,
    output_bias,
    upsample_weight,
    upsample_bias,
):
    row_count, frame_count, col_count, channels = latents.shape
    first_row = lax.axis_index("tile") * row_count
    canvas_onehot, canvas_widths = video_lookup(row_video, video_cols)
    counts = (
        jnp.sum(canvas_onehot, axis=0) * video_cols.astype(jnp.float32) * (channels // GROUPS)
    )[None, :, None]
    bordered = jnp.pad(row_video, 1, constant_values=-1)
    near_labels = lax.dynamic_slice_in_dim(bordered, first_row, row_count + 2)
    own_labels = near_labels[1 : row_count + 1]
    onehot, own_widths = video_lookup(own_labels, video_cols)
    column_ids = jnp.arange(col_count, dtype=jnp.int32)
    valid_mask = column_ids[None, :] < own_widths[:, None]
    mask_four = valid_mask[:, None, :, None]
    source = latents.astype(jnp.float32)
    first_normed = group_norm(source, first_gain, first_shift, onehot, valid_mask, counts)
    hidden = jnp.where(mask_four, jax.nn.silu(first_normed), 0.0).astype(jnp.bfloat16)
    context = causal_context(hidden)
    branch = conv_taps(context, conv_weight, near_labels, own_labels)
    after_conv = jnp.where(mask_four, source + branch + conv_bias, 0.0).astype(jnp.bfloat16)
    second_normed = jnp.where(
        mask_four,
        group_norm(
            after_conv.astype(jnp.float32), second_gain, second_shift, onehot, valid_mask, counts
        ),
        0.0,
    ).astype(jnp.bfloat16)
    flat_normed = second_normed.reshape(-1, channels)
    scale = channels ** (-0.5)
    lowest = own_labels[0]
    highest = own_labels[row_count - 1]
    block_rows = row_count
    while block_rows * col_count < 1024:
        block_rows = block_rows * 2

    def split_pairs(block):
        return (block[..., :channels], block[..., channels:])

    def attend_block(state, block, block_first, project, queries):
        rows_here = block.shape[0]
        block_labels = lax.dynamic_slice_in_dim(row_video, block_first, rows_here)
        block_widths = lax.dynamic_slice_in_dim(canvas_widths, block_first, rows_here)

        def update(carried):
            running_max, running_total, accum = carried
            key_block, value_block = project(block)
            key_flat = jnp.moveaxis(key_block, 1, 0).reshape(frame_count, -1, channels)
            value_flat = jnp.moveaxis(value_block, 1, 0).reshape(frame_count, -1, channels)
            scores = (
                jnp.einsum("rfwc,fkc->rfwk", queries, key_flat, preferred_element_type=jnp.float32)
                * scale
            )
            same_video = own_labels[:, None] == block_labels[None, :]
            key_valid = column_ids[None, :] < block_widths[:, None]
            allowed = (same_video[:, :, None] & key_valid[None, :, :]).reshape(row_count, -1)[
                :, None, None, :
            ]
            scores = jnp.where(allowed, scores, MASKED)
            new_max = jnp.maximum(running_max, jnp.max(scores, axis=3))
            weights = jnp.where(allowed, jnp.exp(scores - new_max[..., None]), 0.0)
            factor = jnp.exp(running_max - new_max)
            running_total = running_total * factor + jnp.sum(weights, axis=3)
            accum = accum * factor[..., None] + jnp.einsum(
                "rfwk,fkc->rfwc",
                weights.astype(jnp.bfloat16),
                value_flat,
                preferred_element_type=jnp.float32,
            )
            return (new_max, running_total, accum)

        def unchanged(carried):
            return carried

        touches = (block_labels[rows_here - 1] >= lowest) & (block_labels[0] <= highest)
        return lax.cond(touches, update, unchanged, state)

    initial = (
        jnp.full((row_count, frame_count, col_count), MASKED, jnp.float32),
        jnp.zeros((row_count, frame_count, col_count), jnp.float32),
        jnp.zeros((row_count, frame_count, col_count, channels), jnp.float32),
    )
    triple = (
        jnp.dot(flat_normed, triple_weight, preferred_element_type=jnp.float32) + triple_bias
    ).astype(jnp.bfloat16)
    triple = triple.reshape(row_count, frame_count, col_count, 3 * channels)
    queries = triple[..., :channels]
    shard_piece = lax.all_gather(triple[..., channels:], "tile", axis=0, tiled=True)
    piece_rows = shard_piece.shape[0]
    step_rows = block_rows

    def advance(position, carried):
        offset = position * step_rows
        block = lax.dynamic_slice_in_dim(shard_piece, offset, step_rows)
        return attend_block(carried, block, offset, split_pairs, queries)

    folded = lax.fori_loop(0, piece_rows // step_rows, advance, initial)
    running_max, running_total, accum = folded
    mixed = (accum / running_total[..., None]).astype(jnp.bfloat16)
    attended = jnp.dot(
        mixed.reshape(-1, channels), output_weight, preferred_element_type=jnp.float32
    ).reshape(row_count, frame_count, col_count, channels)
    after_attention = jnp.where(
        mask_four, after_conv.astype(jnp.float32) + attended + output_bias, 0.0
    ).astype(jnp.bfloat16)
    rimmed = padded_2(after_attention, (("tile", 0),), 1)
    decoded = upsample_conv(rimmed, upsample_weight, near_labels, own_labels)
    up_valid = (
        jnp.arange(2 * col_count, dtype=jnp.int32)[None, :] < 2 * jnp.repeat(own_widths, 2)[:, None]
    )
    return jnp.where(up_valid[:, None, :, None], decoded + upsample_bias, 0.0).astype(jnp.bfloat16)


def solution(mesh):
    in_specs = (
        P("tile", "frame", None, None),
        P(),
        P(),
        P(),
        P(),
        P(),
        P(),
        P(),
        P(),
        P(),
        P(),
        P(),
        P(),
        P(),
        P(),
    )
    out_specs = P("tile", "frame", None, None)
    return jax.shard_map(shards, mesh=mesh, in_specs=in_specs, out_specs=out_specs, check_vma=False)
```

profile of v0, /device:TPU:66, one launch (start us, length us, event | category | flops | bytes accessed | tf_op | source)
XLA Modules:
  0.0 925.6 jit_solution(16521452658198626136)
XLA Ops:
  9.1 1.1 fusion.40
  10.8 71.9 %psum.28 = f32[1,4,32]{2,1,0:T(4,128)S(1)} all-reduce(f32[1,4,32]{2,1,0:T(4,128)S(1)} %convolution_bitcast_fusion.4), channel_id=1, replica_groups=mesh['tile'=32,'frame'=8] {'tile'}, use_global_device_ids=true, to_apply=%region_2.3 | all-reduce | flops 128 | bytes 1024 | tf_op jit(solution)/shard_map/psum | solution.py:50
  83.8 1.1 fusion.44
  85.5 77.4 %psum.29 = f32[1,4,32]{2,1,0:T(4,128)S(1)} all-reduce(f32[1,4,32]{2,1,0:T(4,128)S(1)} %convolution_bitcast_fusion.3), channel_id=1, replica_groups=mesh['tile'=32,'frame'=8] {'tile'}, use_global_device_ids=true, to_apply=%region_5.6 | all-reduce | flops 128 | bytes 1024 | tf_op jit(solution)/shard_map/psum | solution.py:56
  163.4 1.3 select_convert_fusion
  164.7 2.8 collective-permute-start
  167.5 1.9 collective-permute-start.1
  169.5 6.3 collective-permute-done
  175.8 2.2 collective-permute-done.1
  178.1 7.6 collective-permute-start.2
  185.8 6.2 collective-permute-start.3
  192.0 3.9 fusion.117
  197.5 1.2 select_maximum_fusion
  208.7 76.9 %psum.30 = f32[1,4,32]{2,1,0:T(4,128)S(1)} all-reduce(f32[1,4,32]{2,1,0:T(4,128)S(1)} %convolution_bitcast_fusion.2), channel_id=1, replica_groups=mesh['tile'=32,'frame'=8] {'tile'}, use_global_device_ids=true, to_apply=%region_7.8 | all-reduce | flops 128 | bytes 1024 | tf_op jit(solution)/shard_map/psum | solution.py:50
  286.8 79.4 %psum.31 = f32[1,4,32]{2,1,0:T(4,128)S(1)} all-reduce(f32[1,4,32]{2,1,0:T(4,128)S(1)} %convolution_bitcast_fusion.1), channel_id=1, replica_groups=mesh['tile'=32,'frame'=8] {'tile'}, use_global_device_ids=true, to_apply=%region_9.10 | all-reduce | flops 128 | bytes 1024 | tf_op jit(solution)/shard_map/psum | solution.py:56
  372.0 446.9 %all-gather.2.cloned.1.call-done = bf16[128,1,104,768]{3,2,1,0:T(8,128)(2,1)} async-done(((bf16[4,1,104,768]{3,2,1,0:T(8,128)(2,1)}), bf16[128,1,104,768]{3,2,1,0:T(8,128)(2,1)}) %all-gather.2.cloned.1.call-update) | async-done | bytes 20447248 | tf_op jit(solution)/shard_map/all_gather | solution.py:224
  819.1 65.0 %while.18 = (s32[]{:T(128)}, f32[4,1,104]{2,0,1:T(4,128)S(1)}, f32[4,1,104]{2,0,1:T(4,128)S(1)}, f32[4,1,104,384]{3,2,0,1:T(8,128)S(1)}, s32[128]{0:T(128)S(1)},...) while((s32[]{:T(128)}, f32[4,1,104]{2,0,1:T(4,128)S(1)}, ...), condition=%wide.region_16.17_spmd.clone, body=%wide.region_11.16_spmd.clone.sunk | while | flops 1069815168 | bytes 17710040 | solution.py:233
  825.5 5.6 conditional.3
  826.2 2.0 constant_dynamic-slice_fusion.1
  829.9 1.2 fusion.15
  834.3 5.6 conditional.3
  835.0 2.0 constant_dynamic-slice_fusion.1
  838.8 1.2 fusion.15
  843.2 5.6 conditional.3
  843.8 2.0 constant_dynamic-slice_fusion.1
  847.6 1.2 fusion.15
  852.0 5.6 conditional.3
  852.7 2.0 constant_dynamic-slice_fusion.1
  856.4 1.2 fusion.15
  860.8 5.6 conditional.3
  861.5 2.0 constant_dynamic-slice_fusion.1
  865.2 1.2 fusion.15
  869.6 5.6 conditional.3
  870.3 2.0 constant_dynamic-slice_fusion.1
  874.1 1.2 fusion.15
  878.5 5.6 conditional.3
  879.1 2.0 constant_dynamic-slice_fusion.1
  882.9 1.2 fusion.15
  884.6 2.6 collective-permute-start.4
  887.2 6.3 collective-permute-start.5
  896.4 1.4 concatenate.69
  898.9 2.0 broadcast_in_dim.171
  900.9 3.7 broadcast_in_dim.172
  909.2 1.4 fusion.21
  910.7 1.4 convolution_add_fusion.2
  912.1 1.4 convolution_add_fusion.1
  913.5 2.3 reshape.457
  915.8 2.9 fusion.30
  (255 shorter events, 55.0 us)
Async XLA Ops:
  6.5 360.5 %copy-start = (bf16[384,1152]{1,0:T(8,128)(2,1)S(1)}, bf16[384,1152]{1,0:T(8,128)(2,1)}, u32[]{:S(2)}) copy-start(bf16[384,1152]{1,0:T(8,128)(2,1)} %param.28) | copy-start | bytes 2654212
  6.5 812.4 %all-gather.2.cloned.1.call-start = ((), (), s32[]{:S(2)}) async-start(), calls=%async_computation | async-start | bytes 21086208 | tf_op jit(solution)/shard_map/all_gather | solution.py:224
  164.7 11.1 %collective-permute-start = (bf16[4,1,104,384]{3,2,0,1:T(8,128)(2,1)S(1)}, bf16[4,1,104,384]{3,2,0,1:T(8,128)(2,1)S(1)}, u32[]{:S(2)}, u32[]{:S(2)}) collective-permute-start(bf16[4,1,104,384]{3,2,0,1:T(8,128)(2,1)S(1)} %select_convert_fusion), channel_id=1, source_target_pairs={{0,2},{1,3},{2,4},{3,5},{4,6},{5,7},{8,10},{9,11},{10,12},{11,13},... | collective-permute-start | bytes 958472 | tf_op jit(solution)/shard_map/ppermute | solution.py:17
  167.5 10.5 %collective-permute-start.1 = (bf16[4,1,104,384]{3,2,0,1:T(8,128)(2,1)S(1)}, bf16[4,1,104,384]{3,2,0,1:T(8,128)(2,1)S(1)}, u32[]{:S(2)}, u32[]{:S(2)}) collective-permute-start(bf16[4,1,104,384]{3,2,0,1:T(8,128)(2,1)S(1)} %select_convert_fusion), channel_id=1, source_target_pairs={{0,1},{1,2},{2,3},{3,4},{4,5},{5,6},{6,7},{8,9},{9,10},{10,11},{11... | collective-permute-start | bytes 958472 | tf_op jit(solution)/shard_map/ppermute | solution.py:17
  178.1 18.5 %collective-permute-start.2 = (bf16[1,3,104,384]{3,2,0,1:T(8,128)(2,1)S(1)}, bf16[1,3,104,384]{3,2,0,1:T(8,128)(2,1)S(1)}, u32[]{:S(2)}, u32[]{:S(2)}) collective-permute-start(bf16[1,3,104,384]{3,2,0,1:T(8,128)(2,1)S(1)} %get-tuple-element.417), channel_id=1, source_target_pairs={{0,8},{8,16},{16,24},{24,32},{32,40},{40,48},{48,56},{56,64},{64,7... | collective-permute-start | bytes 718856 | tf_op jit(solution)/shard_map/ppermute | solution.py:27
  185.8 11.7 %collective-permute-start.3 = (bf16[1,3,104,384]{3,2,0,1:T(8,128)(2,1)S(1)}, bf16[1,3,104,384]{3,2,0,1:T(8,128)(2,1)S(1)}, u32[]{:S(2)}, u32[]{:S(2)}) collective-permute-start(bf16[1,3,104,384]{3,2,0,1:T(8,128)(2,1)S(1)} %get-tuple-element.418), channel_id=1, source_target_pairs={{8,0},{16,8},{24,16},{32,24},{40,32},{48,40},{56,48},{64,56},{72,6... | collective-permute-start | bytes 718856 | tf_op jit(solution)/shard_map/ppermute | solution.py:28
  206.9 1.0 copy-start.2
  207.0 1.0 copy-start.7
  207.0 159.8 %copy-start.8 = (f32[384]{0:T(512)S(1)}, f32[384]{0:T(512)}, u32[]{:S(2)}) copy-start(f32[384]{0:T(512)} %param.27) | copy-start | bytes 4612
  207.0 159.8 %copy-start.9 = (f32[384]{0:T(512)S(1)}, f32[384]{0:T(512)}, u32[]{:S(2)}) copy-start(f32[384]{0:T(512)} %param.26) | copy-start | bytes 4612
  207.7 159.3 %copy-start.12 = (f32[1152]{0:T(1024)S(1)}, f32[1152]{0:T(1024)}, u32[]{:S(2)}) copy-start(f32[1152]{0:T(1024)} %param.29) | copy-start | bytes 13828
  367.0 3.7 copy-start.14
  367.0 3.7 copy-start.15
  367.0 3.8 copy-start.3
  367.7 1.0 copy-start.5
  819.0 65.0 %copy-start.11 = (bf16[384,384]{1,0:T(8,128)(2,1)S(1)}, bf16[384,384]{1,0:T(8,128)(2,1)}, u32[]{:S(2)}) copy-start(bf16[384,384]{1,0:T(8,128)(2,1)} %param.30) | copy-start | bytes 884740
  819.1 65.0 %copy-start.13 = (f32[384]{0:T(512)S(1)}, f32[384]{0:T(512)}, u32[]{:S(2)}) copy-start(f32[384]{0:T(512)} %param.31) | copy-start | bytes 4612
  884.6 13.2 %collective-permute-start.4 = (bf16[1,1,104,384]{3,2,0,1:T(8,128)(2,1)S(1)}, bf16[1,1,104,384]{3,2,0,1:T(8,128)(2,1)S(1)}, u32[]{:S(2)}, u32[]{:S(2)}) collective-permute-start(bf16[1,1,104,384]{3,2,0,1:T(8,128)(2,1)S(1)} %get-tuple-element.437), channel_id=1, source_target_pairs={{0,8},{8,16},{16,24},{24,32},{32,40},{40,48},{48,56},{56,64},{64,7... | collective-permute-start | bytes 239624 | tf_op jit(solution)/shard_map/ppermute | solution.py:27
  887.2 10.6 %collective-permute-start.5 = (bf16[1,1,104,384]{3,2,0,1:T(8,128)(2,1)S(1)}, bf16[1,1,104,384]{3,2,0,1:T(8,128)(2,1)}, u32[]{:S(2)}, u32[]{:S(2)}) collective-permute-start(bf16[1,1,104,384]{3,2,0,1:T(8,128)(2,1)S(1)} %get-tuple-element.438), channel_id=1, source_target_pairs={{8,0},{16,8},{24,16},{32,24},{40,32},{48,40},{56,48},{64,56},{72,6... | collective-permute-start | bytes 239624 | tf_op jit(solution)/shard_map/ppermute | solution.py:28
  907.8 1.3 copy-start.4
  907.9 1.4 copy-start.6
  912.1 6.6 copy-start.1
  913.5 2.3 copy-start.10
Sparse Core Ops, SparseCore 0:
  369.7 449.2 all-gather.1
where the time goes:
time: 928 us; the launch traced here: 926 us
  waiting for transfers between devices  457 us (49%)
  blocking collectives  306 us (33%)
  local copies, waits for them, and re-layouts  48.7 us (5%)
  matrix products  31.5 us (3%)
  starting transfers between devices  27.4 us (3%)
  loops' own time  21 us (2%)
  other arithmetic  20.3 us (2%)
  between operations  14 us (2%)
    all_gather x1, waiting for transfers between devices, shards(): lax.all_gather(triple[..., channels:], 'tile', axis=0, tiled=True)  447 us
    psum x2, blocking collectives, group_norm(): variance = lax.psum(partial_spread, 'tile') / counts  157 us
    psum x2, blocking collectives, group_norm(): group_mean = lax.psum(partial_sum, 'tile') / counts  149 us
    another operation x1, loops' own time, shards(): folded = lax.fori_loop(0, piece_rows // step_rows, advance, initial)  20.3 us
  transfers between devices with their start and end apart: 7, of which 5 were waited for; matrix products, arithmetic and copies ran while one was open for 1% of the time, Pallas kernels for 0%

commit v1 on v0

--- a/solution.py
+++ b/solution.py
@@ -170,22 +170,17 @@
     while block_rows * col_count < 1024:
         block_rows = block_rows * 2
 
-    def split_pairs(block):
-        return (block[..., :channels], block[..., channels:])
-
-    def attend_block(state, block, block_first, project, queries):
+    def attend_block(state, block, block_first, queries, query_shift):
         rows_here = block.shape[0]
         block_labels = lax.dynamic_slice_in_dim(row_video, block_first, rows_here)
         block_widths = lax.dynamic_slice_in_dim(canvas_widths, block_first, rows_here)
 
         def update(carried):
             running_max, running_total, accum = carried
-            key_block, value_block = project(block)
-            key_flat = jnp.moveaxis(key_block, 1, 0).reshape(frame_count, -1, channels)
-            value_flat = jnp.moveaxis(value_block, 1, 0).reshape(frame_count, -1, channels)
+            cells_flat = jnp.moveaxis(block, 1, 0).reshape(frame_count, -1, channels)
             scores = (
-                jnp.einsum("rfwc,fkc->rfwk", queries, key_flat, preferred_element_type=jnp.float32)
-                * scale
+                jnp.einsum("rfwc,fkc->rfwk", queries, cells_flat, preferred_element_type=jnp.float32)
+                + query_shift[..., None]
             )
             same_video = own_labels[:, None] == block_labels[None, :]
             key_valid = column_ids[None, :] < block_widths[:, None]
@@ -200,7 +195,7 @@
             accum = accum * factor[..., None] + jnp.einsum(
                 "rfwk,fkc->rfwc",
                 weights.astype(jnp.bfloat16),
-                value_flat,
+                cells_flat,
                 preferred_element_type=jnp.float32,
             )
             return (new_max, running_total, accum)
@@ -216,23 +211,38 @@
         jnp.zeros((row_count, frame_count, col_count), jnp.float32),
         jnp.zeros((row_count, frame_count, col_count, channels), jnp.float32),
     )
-    triple = (
-        jnp.dot(flat_normed, triple_weight, preferred_element_type=jnp.float32) + triple_bias
-    ).astype(jnp.bfloat16)
-    triple = triple.reshape(row_count, frame_count, col_count, 3 * channels)
-    queries = triple[..., :channels]
-    shard_piece = lax.all_gather(triple[..., channels:], "tile", axis=0, tiled=True)
+    key_weight = triple_weight[:, channels : 2 * channels]
+    value_weight = triple_weight[:, 2 * channels :]
+    plain = (
+        jnp.dot(flat_normed, triple_weight[:, :channels], preferred_element_type=jnp.float32)
+        + triple_bias[:channels]
+    ).astype(jnp.bfloat16)
+    query_shift = (
+        jnp.dot(plain.astype(jnp.float32), triple_bias[channels : 2 * channels], precision=HIGHEST)
+        * scale
+    ).reshape(row_count, frame_count, col_count)
+    queries = (
+        jnp.einsum("nd,cd->nc", plain, key_weight, preferred_element_type=jnp.float32) * scale
+    ).astype(jnp.bfloat16)
+    queries = queries.reshape(row_count, frame_count, col_count, channels)
+    shard_piece = lax.all_gather(second_normed, "tile", axis=0, tiled=True)
     piece_rows = shard_piece.shape[0]
     step_rows = block_rows
 
     def advance(position, carried):
         offset = position * step_rows
         block = lax.dynamic_slice_in_dim(shard_piece, offset, step_rows)
-        return attend_block(carried, block, offset, split_pairs, queries)
+        return attend_block(carried, block, offset, queries, query_shift)
 
     folded = lax.fori_loop(0, piece_rows // step_rows, advance, initial)
     running_max, running_total, accum = folded
-    mixed = (accum / running_total[..., None]).astype(jnp.bfloat16)
+    averaged = (accum / running_total[..., None]).astype(jnp.bfloat16)
+    mixed = (
+        jnp.dot(
+            averaged.reshape(-1, channels), value_weight, preferred_element_type=jnp.float32
+        )
+        + triple_bias[2 * channels :]
+    ).astype(jnp.bfloat16)
     attended = jnp.dot(
         mixed.reshape(-1, channels), output_weight, preferred_element_type=jnp.float32
     ).reshape(row_count, frame_count, col_count, channels)

time: 928 us -> 709 us (0.76)
  waiting for transfers between devices: 457 us -> 242 us
  starting transfers between devices: 27.4 us -> 52.7 us
  local copies, waits for them, and re-layouts: 48.7 us -> 29.4 us
    all_gather x1, waiting for transfers between devices: 447 us -> 232 us  [shards(): shard_piece = lax.all_gather(second_normed, 'tile', axis=0, tiled=True)]
    ppermute x2, starting transfers between devices: 10.2 us -> 39.9 us  [padded_2(): before = lax.ppermute(last, axis, up)]
    slice x9 -> x2, local copies, waits for them, and re-layouts: 15.6 us -> 0.01 us  [the longest x1 0.01 us: shards(): triple_bias[2 * channels:]]
  transfers between devices with their start and end apart: 7 -> 7, of which waited for: 5 -> 5; matrix products, arithmetic and copies ran while one was open for 1% -> 2% of each run, Pallas kernels for 0% -> 0%
where the time goes in v1:
time: 709 us; the launch traced here: 707 us
  blocking collectives  306 us (43%)
  waiting for transfers between devices  242 us (34%)
  starting transfers between devices  52.7 us (7%)
  local copies, waits for them, and re-layouts  29.4 us (4%)
  matrix products  26.3 us (4%)
  loops' own time  21.1 us (3%)
  other arithmetic  15.2 us (2%)
  between operations  14 us (2%)
    all_gather x1, waiting for transfers between devices, shards(): shard_piece = lax.all_gather(second_normed, 'tile', axis=0, tiled=True)  232 us
    psum x2, blocking collectives, group_norm(): variance = lax.psum(partial_spread, 'tile') / counts  157 us
    psum x2, blocking collectives, group_norm(): group_mean = lax.psum(partial_sum, 'tile') / counts  149 us
    ppermute x2, starting transfers between devices, padded_2(): before = lax.ppermute(last, axis, up)  39.9 us
    another operation x1, loops' own time, shards(): folded = lax.fori_loop(0, piece_rows // step_rows, advance, initial)  20.8 us
  transfers between devices with their start and end apart: 7, of which 5 were waited for; matrix products, arithmetic and copies ran while one was open for 2% of the time, Pallas kernels for 0%

profile of v1, /device:TPU:66, one launch (start us, length us, event | category | flops | bytes accessed | tf_op | source)
XLA Modules:
  0.0 706.6 jit_solution(15514580135167725214)
XLA Ops:
  6.6 0.8 convert_reduce_fusion
  7.4 0.7 pad_dynamic-slice_fusion
  8.2 0.8 select_reduce_fusion.1
  9.1 1.1 fusion.40
  10.7 71.9 %psum.28 = f32[1,4,32]{2,1,0:T(4,128)S(1)} all-reduce(f32[1,4,32]{2,1,0:T(4,128)S(1)} %convolution_bitcast_fusion.4), channel_id=1, replica_groups=mesh['tile'=32,'frame'=8] {'tile'}, use_global_device_ids=true, to_apply=%region_2.3 | all-reduce | flops 128 | bytes 1024 | tf_op jit(solution)/shard_map/psum | solution.py:50
  83.8 1.1 fusion.44
  85.4 77.4 %psum.29 = f32[1,4,32]{2,1,0:T(4,128)S(1)} all-reduce(f32[1,4,32]{2,1,0:T(4,128)S(1)} %convolution_bitcast_fusion.3), channel_id=1, replica_groups=mesh['tile'=32,'frame'=8] {'tile'}, use_global_device_ids=true, to_apply=%region_5.6 | all-reduce | flops 128 | bytes 1024 | tf_op jit(solution)/shard_map/psum | solution.py:56
  163.3 1.3 select_convert_fusion
  164.7 2.8 collective-permute-start
  167.5 1.9 collective-permute-start.1
  169.4 6.3 collective-permute-done
  175.8 2.2 collective-permute-done.1
  178.1 7.6 %collective-permute-start.2 = (bf16[1,3,104,384]{3,2,1,0:T(8,128)(2,1)S(1)}, bf16[1,3,104,384]{3,2,1,0:T(8,128)(2,1)S(1)}, u32[]{:S(2)}, u32[]{:S(2)}) collective-permute-start(bf16[1,3,104,384]{3,2,1,0:T(8,128)(2,1)S(1)} %get-tuple-element.443), channel_id=1, source_target_pairs={{0,8},{8,16},{16,24},{24,32},{32,40},{40,48},{48,56},{56,64},{64,7... | collective-permute-start | bytes 718856 | tf_op jit(solution)/shard_map/ppermute | solution.py:27
  185.7 6.2 collective-permute-start.3
  191.9 3.8 fusion.123
  196.6 0.9 collective-permute-done.3
  197.5 1.3 select_maximum_fusion
  208.7 76.9 %psum.30 = f32[1,4,32]{2,1,0:T(4,128)S(1)} all-reduce(f32[1,4,32]{2,1,0:T(4,128)S(1)} %convolution_bitcast_fusion.2), channel_id=1, replica_groups=mesh['tile'=32,'frame'=8] {'tile'}, use_global_device_ids=true, to_apply=%region_7.8 | all-reduce | flops 128 | bytes 1024 | tf_op jit(solution)/shard_map/psum | solution.py:50
  286.8 79.4 %psum.31 = f32[1,4,32]{2,1,0:T(4,128)S(1)} all-reduce(f32[1,4,32]{2,1,0:T(4,128)S(1)} %convolution_bitcast_fusion.1), channel_id=1, replica_groups=mesh['tile'=32,'frame'=8] {'tile'}, use_global_device_ids=true, to_apply=%region_9.10 | all-reduce | flops 128 | bytes 1024 | tf_op jit(solution)/shard_map/psum | solution.py:56
  366.8 1.0 fusion.58
  369.1 0.9 fusion.125
  370.0 1.3 fusion.36
  371.7 2.1 fusion.37
  373.8 232.0 %all-gather.2.cloned.1.call-done = bf16[128,1,104,384]{3,2,1,0:T(8,128)(2,1)} async-done(((bf16[4,1,104,384]{3,2,1,0:T(8,128)(2,1)}), bf16[128,1,104,384]{3,2,1,0:T(8,128)(2,1)}) %all-gather.2.cloned.1.call-update) | async-done | bytes 10223632 | tf_op jit(solution)/shard_map/all_gather | solution.py:228
  605.8 38.6 %while.18 = (s32[]{:T(128)}, f32[4,1,104]{2,0,1:T(4,128)S(1)}, f32[4,1,104]{2,0,1:T(4,128)S(1)}, f32[4,1,104,384]{3,2,0,1:T(8,128)S(1)}, s32[128]{0:T(128)S(1)},...) while((s32[]{:T(128)}, f32[4,1,104]{2,0,1:T(4,128)S(1)}, ...), condition=%wide.region_16.17_spmd.clone, body=%wide.region_11.16_spmd.clone.sunk | while | flops 1069815168 | bytes 15159129 | solution.py:237
  612.3 6.1 conditional.3
  613.0 1.4 constant_dynamic-slice_fusion
  614.5 2.1 fusion.121
  617.3 1.1 fusion.16
  621.7 6.1 conditional.3
  622.4 1.4 constant_dynamic-slice_fusion
  623.9 2.1 fusion.121
  626.7 1.1 fusion.16
  644.6 1.6 fusion.39
  646.4 32.2 %collective-permute-start.4 = (bf16[1,1,104,384]{3,2,1,0:T(8,128)(2,1)S(1)}, bf16[1,1,104,384]{3,2,1,0:T(8,128)(2,1)S(1)}, u32[]{:S(2)}, u32[]{:S(2)}) collective-permute-start(bf16[1,1,104,384]{3,2,1,0:T(8,128)(2,1)S(1)} %get-tuple-element.463), channel_id=1, source_target_pairs={{0,8},{8,16},{16,24},{24,32},{32,40},{40,48},{48,56},{56,64},{64,7... | collective-permute-start | bytes 239624 | tf_op jit(solution)/shard_map/ppermute | solution.py:27
  678.6 1.9 collective-permute-start.5
  681.0 0.8 copy.40
  682.2 0.8 copy.39
  683.4 0.8 copy.41
  685.0 1.4 concatenate.69
  686.6 0.8 broadcast_in_dim.172
  688.7 0.9 slice_multiply_fusion
  691.8 0.9 copy-done.6
  692.8 1.4 fusion.22
  694.2 1.4 convolution_add_fusion.1
  695.6 1.4 convolution_add_fusion
  697.1 1.1 reshape.456
  698.2 1.5 fusion.30
  (179 shorter events, 31.1 us)
Async XLA Ops:
  6.5 638.0 %copy-start = (bf16[384,384]{1,0:T(8,128)(2,1)S(1)}, bf16[384,384]{1,0:T(8,128)(2,1)}, u32[]{:S(2)}) copy-start(bf16[384,384]{1,0:T(8,128)(2,1)} %param.30) | copy-start | bytes 884740
  6.5 599.2 %all-gather.2.cloned.1.call-start = ((), (), s32[]{:S(2)}) async-start(), calls=%async_computation | async-start | bytes 10543104 | tf_op jit(solution)/shard_map/all_gather | solution.py:228
  164.7 11.1 %collective-permute-start = (bf16[4,1,104,384]{3,2,1,0:T(8,128)(2,1)S(1)}, bf16[4,1,104,384]{3,2,1,0:T(8,128)(2,1)S(1)}, u32[]{:S(2)}, u32[]{:S(2)}) collective-permute-start(bf16[4,1,104,384]{3,2,1,0:T(8,128)(2,1)S(1)} %select_convert_fusion), channel_id=1, source_target_pairs={{0,2},{1,3},{2,4},{3,5},{4,6},{5,7},{8,10},{9,11},{10,12},{11,13},... | collective-permute-start | bytes 958472 | tf_op jit(solution)/shard_map/ppermute | solution.py:17
  167.5 10.5 %collective-permute-start.1 = (bf16[4,1,104,384]{3,2,1,0:T(8,128)(2,1)S(1)}, bf16[4,1,104,384]{3,2,1,0:T(8,128)(2,1)S(1)}, u32[]{:S(2)}, u32[]{:S(2)}) collective-permute-start(bf16[4,1,104,384]{3,2,1,0:T(8,128)(2,1)S(1)} %select_convert_fusion), channel_id=1, source_target_pairs={{0,1},{1,2},{2,3},{3,4},{4,5},{5,6},{6,7},{8,9},{9,10},{10,11},{11... | collective-permute-start | bytes 958472 | tf_op jit(solution)/shard_map/ppermute | solution.py:17
  178.1 18.5 %collective-permute-start.2 = (bf16[1,3,104,384]{3,2,1,0:T(8,128)(2,1)S(1)}, bf16[1,3,104,384]{3,2,1,0:T(8,128)(2,1)S(1)}, u32[]{:S(2)}, u32[]{:S(2)}) collective-permute-start(bf16[1,3,104,384]{3,2,1,0:T(8,128)(2,1)S(1)} %get-tuple-element.443), channel_id=1, source_target_pairs={{0,8},{8,16},{16,24},{24,32},{32,40},{40,48},{48,56},{56,64},{64,7... | collective-permute-start | bytes 718856 | tf_op jit(solution)/shard_map/ppermute | solution.py:27
  185.7 11.7 %collective-permute-start.3 = (bf16[1,3,104,384]{3,2,1,0:T(8,128)(2,1)S(1)}, bf16[1,3,104,384]{3,2,1,0:T(8,128)(2,1)S(1)}, u32[]{:S(2)}, u32[]{:S(2)}) collective-permute-start(bf16[1,3,104,384]{3,2,1,0:T(8,128)(2,1)S(1)} %get-tuple-element.444), channel_id=1, source_target_pairs={{8,0},{16,8},{24,16},{32,24},{40,32},{48,40},{56,48},{64,56},{72,6... | collective-permute-start | bytes 718856 | tf_op jit(solution)/shard_map/ppermute | solution.py:28
  206.9 1.0 copy-start.1
  207.0 1.0 copy-start.10
  207.0 159.8 %copy-start.11 = (f32[384]{0:T(512)S(1)}, f32[384]{0:T(512)}, u32[]{:S(2)}) copy-start(f32[384]{0:T(512)} %param.27) | copy-start | bytes 4612
  207.0 159.8 %copy-start.12 = (f32[384]{0:T(512)S(1)}, f32[384]{0:T(512)}, u32[]{:S(2)}) copy-start(f32[384]{0:T(512)} %param.26) | copy-start | bytes 4612
  207.7 160.1 %copy-start.9 = (f32[1152]{0:T(1024)S(1)}, f32[1152]{0:T(1024)}, u32[]{:S(2)}) copy-start(f32[1152]{0:T(1024)} %param.29) | copy-start | bytes 13828
  207.7 161.2 %copy-start.15 = (s32[4]{0:T(128)S(1)}, s32[4]{0:T(128)}, u32[]{:S(2)}) copy-start(s32[4]{0:T(128)} %param.21) | copy-start | bytes 52
  207.7 161.2 %copy-start.16 = (s32[128]{0:T(128)S(1)}, s32[128]{0:T(128)}, u32[]{:S(2)}) copy-start(s32[128]{0:T(128)} %param.20) | copy-start | bytes 1540
  207.9 161.2 %copy-start.5 = (bf16[3,3,384,192]{2,3,1,0:T(8,128)(2,1)S(1)}, bf16[3,3,384,192]{2,3,1,0:T(8,128)(2,1)}, u32[]{:S(2)}) copy-start(bf16[3,3,384,192]{2,3,1,0:T(8,128)(2,1)} %param.32) | copy-start | bytes 3981316
  368.3 1.7 copy-start.7
  644.4 1.8 copy-start.13
  644.5 36.1 %copy-start.2 = (bf16[1,3,384,192]{2,3,1,0:T(8,128)(2,1)S(1)}, bf16[1,3,384,192]{2,3,1,0:T(8,128)(2,1)}, u32[]{:S(2)}) copy-start(bf16[1,3,384,192]{2,3,1,0:T(8,128)(2,1)} %get-tuple-element.436) | copy-start | bytes 1327108
  646.4 40.0 %collective-permute-start.4 = (bf16[1,1,104,384]{3,2,1,0:T(8,128)(2,1)S(1)}, bf16[1,1,104,384]{3,2,1,0:T(8,128)(2,1)S(1)}, u32[]{:S(2)}, u32[]{:S(2)}) collective-permute-start(bf16[1,1,104,384]{3,2,1,0:T(8,128)(2,1)S(1)} %get-tuple-element.463), channel_id=1, source_target_pairs={{0,8},{8,16},{16,24},{24,32},{32,40},{40,48},{48,56},{56,64},{64,7... | collective-permute-start | bytes 239624 | tf_op jit(solution)/shard_map/ppermute | solution.py:27
  678.6 7.7 %collective-permute-start.5 = (bf16[1,1,104,384]{3,2,1,0:T(8,128)(2,1)S(1)}, bf16[1,1,104,384]{3,2,1,0:T(8,128)(2,1)S(1)}, u32[]{:S(2)}, u32[]{:S(2)}) collective-permute-start(bf16[1,1,104,384]{3,2,1,0:T(8,128)(2,1)S(1)} %get-tuple-element.464), channel_id=1, source_target_pairs={{8,0},{16,8},{24,16},{32,24},{40,32},{48,40},{56,48},{64,56},{72,6... | collective-permute-start | bytes 239624 | tf_op jit(solution)/shard_map/ppermute | solution.py:28
  691.4 1.3 copy-start.6
  691.4 1.4 copy-start.8
  692.8 1.4 copy-start.3
  694.2 1.4 copy-start.4
  697.0 1.2 copy-start.14
Sparse Core Ops, SparseCore 0:
  367.9 237.8 all-gather.1

commit v2 on v0

v2 whole, which is shorter than its diff:
```python
import functools
import math

import jax
import jax.numpy as jnp
import numpy as np
from jax import lax
from jax.experimental import pallas as pl
from jax.experimental.pallas import tpu as pltpu
from jax.sharding import PartitionSpec as P

GROUPS = 32
EPSILON = 1e-05
MASKED = -1e30
HIGHEST = lax.Precision.HIGHEST
MESH = pl.DeviceIdType.MESH
F32 = jnp.float32
BF16 = jnp.bfloat16
CH = 384
OUT = 192
ROWS = 4
COLS = 104
WIDE = 112
CELLS = ROWS * COLS
PADDED = ROWS * WIDE
LAST = CELLS - WIDE
LANES = 128
EXT = CH + LANES
TILES = 32
FRAMES = 8
KEYS = 8 * CELLS
NT = (((1,), (1,)), ((), ()))


def remote(src, dst, send_sem, recv_sem, tile, frame):
    return pltpu.make_async_remote_copy(
        src_ref=src,
        dst_ref=dst,
        send_sem=send_sem,
        recv_sem=recv_sem,
        device_id={"tile": tile, "frame": frame},
        device_id_type=MESH,
    )


def place():
    tile = lax.axis_index("tile")
    frame = lax.axis_index("frame")
    x = lax.div(tile, 8)
    y = lax.rem(lax.div(tile, 2), 4)
    z = lax.rem(tile, 2)
    return tile, frame, x, y, z


def tile_at(x, y, z):
    return lax.rem(x, 4) * 8 + lax.rem(y, 4) * 2 + lax.rem(z, 2)


def greet(barrier, tile, frame):
    pl.semaphore_signal(
        barrier, inc=1, device_id={"tile": tile, "frame": frame}, device_id_type=MESH
    )


def exact(a, b):
    return jnp.dot(a, b, precision=HIGHEST, preferred_element_type=F32)


def pick(table, label):
    rows = lax.broadcasted_iota(jnp.int32, (8, CH), 0)
    chosen = rows == label
    mean = jnp.sum(jnp.where(chosen, table[0:8, :], 0.0), axis=0, keepdims=True)
    scale = jnp.sum(jnp.where(chosen, table[8:16, :], 0.0), axis=0, keepdims=True)
    return mean, scale


def local_sums(values, labels, widths, first, member, member_t, st):
    column = lax.broadcasted_iota(jnp.int32, (COLS, CH), 0)
    line = lax.broadcasted_iota(jnp.int32, (8, 1), 0)
    per_row = jnp.ones((8, 1), F32)
    for r in range(ROWS):
        width = widths[first + r]
        mask = column < width
        cells = values[r * COLS : (r + 1) * COLS]
        total = jnp.sum(jnp.where(mask, cells, 0.0), axis=0, keepdims=True)
        mean = total / width.astype(F32)
        apart = jnp.where(mask, cells - mean, 0.0)
        st[r : r + 1, :] = total
        st[ROWS + r : ROWS + r + 1, :] = jnp.sum(apart * apart, axis=0, keepdims=True)
        per_row = jnp.where((line == r) | (line == ROWS + r), width.astype(F32), per_row)
    upper = line < ROWS
    held = st[...]
    grouped = exact(held, member_t)
    group_mean = exact(jnp.where(upper, grouped / (per_row * (CH // GROUPS)), 0.0), member)
    spread = jnp.where(upper, held / per_row - group_mean, 0.0)
    extra = exact(per_row * spread * spread, member_t)
    lower = pltpu.roll(extra, ROWS, 0)
    return jnp.where(upper, grouped, grouped + lower)


def gather_sums(gat, send_sems, recv_sems):
    tile, frame, x, y, z = place()
    peer = tile_at(x, y, z + 1)
    copy = remote(gat.at[tile], gat.at[tile], send_sems.at[0], recv_sems.at[0], peer, frame)
    copy.start()
    copy.wait()
    mine = pl.ds(tile - z, 2)
    copies = []
    for d in range(1, 4):
        peer = tile_at(x, y + d, z)
        copies.append(
            remote(gat.at[mine], gat.at[mine], send_sems.at[d], recv_sems.at[d], peer, frame)
        )
    for copy in copies:
        copy.start()
    for copy in copies:
        copy.wait()
    mine = pl.ds(x * 8, 8)
    copies = []
    for d in range(1, 4):
        peer = tile_at(x + d, y, z)
        copies.append(
            remote(
                gat.at[mine], gat.at[mine], send_sems.at[3 + d], recv_sems.at[3 + d], peer, frame
            )
        )
    for copy in copies:
        copy.start()
    for copy in copies:
        copy.wait()


def combine_sums(gat, onehot_sum, onehot_sum_t, onehot_both, row_cells, inverse, member):
    held = gat[...].reshape(TILES * 8, LANES)
    mean = exact(onehot_sum, held) * inverse
    mean_rows = exact(onehot_sum_t, mean)
    upper = lax.rem(lax.broadcasted_iota(jnp.int32, (TILES * 8, 1), 0), 8) < ROWS
    off = held / row_cells - mean_rows
    spread = jnp.where(upper, row_cells * off * off, held)
    variance = exact(onehot_both, spread) * inverse
    scale = lax.rsqrt(variance + EPSILON)
    return exact(mean, member), exact(scale, member)


def front_kernel(
    labels, widths, lat, onehot_sum, onehot_sum_t, onehot_both, row_cells, inverse, member,
    member_t, gain, shift, weight_hbm, bias, out,
    main, top, bot, gat, st, tabs, hid, weight, acc,
    stat_send, stat_recv, main_send, main_recv, halo_send, halo_recv, tab_send, tab_recv,
    weight_sem,
):
    tile, frame, x, y, z = place()
    first = tile * ROWS + 1
    load = pltpu.make_async_copy(weight_hbm, weight, weight_sem)
    load.start()
    barrier = pltpu.get_barrier_semaphore()
    greet(barrier, tile_at(x, y, z + 1), frame)
    for d in range(1, 4):
        greet(barrier, tile_at(x, y + d, z), frame)
        greet(barrier, tile_at(x + d, y, z), frame)
    awaited = 7
    for step in (-2, -1, 1, 2):
        there = (frame + step >= 0) & (frame + step < FRAMES)

        @pl.when(there)
        def _():
            greet(barrier, tile, frame + step)

        awaited = awaited + there.astype(jnp.int32)
    for step in (-1, 1):
        there = (tile + step >= 0) & (tile + step < TILES)

        @pl.when(there)
        def _():
            greet(barrier, tile + step, frame)

        awaited = awaited + there.astype(jnp.int32)
    pl.semaphore_wait(barrier, awaited)

    even = lax.rem(frame, 2) == 0
    next_frame = frame + 1 < FRAMES
    skip_frame = even & (frame + 2 < FRAMES)
    relay = even & (frame >= 2)
    has = {1: frame >= 1, 0: frame >= 2}
    above = tile >= 1
    below = tile + 1 < TILES

    to_next = remote(lat, main.at[1], main_send.at[1], main_recv.at[1], tile, frame + 1)
    to_skip = remote(lat, main.at[0], main_send.at[0], main_recv.at[0], tile, frame + 2)
    to_relay = remote(main.at[1], main.at[0], main_send.at[2], main_recv.at[0], tile, frame + 1)

    def halo(a):
        src = lat if a == 2 else main.at[a]
        up = remote(
            src.at[pl.ds(0, WIDE)], bot.at[a], halo_send.at[a, 0], halo_recv.at[a, 0],
            tile - 1, frame,
        )
        down = remote(
            src.at[pl.ds(LAST, WIDE)], top.at[a], halo_send.at[a, 1], halo_recv.at[a, 1],
            tile + 1, frame,
        )
        return up, down

    def start_halo(a):
        up, down = halo(a)

        @pl.when(above)
        def _():
            up.start()

        @pl.when(below)
        def _():
            down.start()

    def wait_halo(a):
        up, down = halo(a)

        @pl.when(below)
        def _():
            up.wait_recv()

        @pl.when(above)
        def _():
            down.wait_recv()

    def end_halo(a):
        up, down = halo(a)

        @pl.when(above)
        def _():
            up.wait_send()

        @pl.when(below)
        def _():
            down.wait_send()

    @pl.when(skip_frame)
    def _():
        to_skip.start()

    @pl.when(next_frame)
    def _():
        to_next.start()

    start_halo(2)

    source = lat[...].astype(F32)
    gat[tile] = local_sums(source, labels, widths, first, member[...], member_t[...], st)
    gather_sums(gat, stat_send, stat_recv)
    mean, scale = combine_sums(
        gat, onehot_sum[...], onehot_sum_t[...], onehot_both[...], row_cells[...], inverse[...],
        member[...],
    )
    tabs[2, 0:8, :] = mean
    tabs[2, 8:16, :] = scale
    tab_next = remote(tabs.at[2], tabs.at[1], tab_send.at[1], tab_recv.at[1], tile, frame + 1)
    tab_skip = remote(tabs.at[2], tabs.at[0], tab_send.at[0], tab_recv.at[0], tile, frame + 2)

    @pl.when(next_frame)
    def _():
        tab_next.start()

    @pl.when(frame + 2 < FRAMES)
    def _():
        tab_skip.start()

    column = lax.broadcasted_iota(jnp.int32, (COLS, CH), 0)

    def activate(a, row, cells):
        label = labels[first - 1 + row]
        width = widths[first - 1 + row]
        row_mean, row_scale = pick(tabs[a], label)
        normed = (cells - row_mean) * row_scale * gain[...] + shift[...]
        hidden = normed / (1.0 + jnp.exp(-normed))
        hidden = jnp.where(column < width, hidden, 0.0)
        hidden = jnp.concatenate([hidden, jnp.zeros((WIDE - COLS, CH), F32)], axis=0)
        lines = pl.ds(row * WIDE, WIDE)
        hid[a, lines, 0:CH] = pltpu.roll(hidden, 1, 0).astype(BF16)
        hid[a, lines, CH : 2 * CH] = hidden.astype(BF16)
        hid[a, lines, 2 * CH : 3 * CH] = pltpu.roll(hidden, WIDE - 1, 0).astype(BF16)

    def activate_main(a):
        cells = lat[...].astype(F32) if a == 2 else main[a].astype(F32)
        for r in range(ROWS):
            activate(a, r + 1, cells[r * COLS : (r + 1) * COLS])

    def activate_halo(a):
        activate(a, 0, top[a].astype(F32)[WIDE - COLS :])
        activate(a, ROWS + 1, bot[a].astype(F32)[:COLS])

    def convolve(a):
        def tap(b, carry):
            lines = pl.ds(pl.multiple_of(b * WIDE, 16), PADDED)
            product = jnp.dot(hid[a, lines, :], weight[a * 3 + b], preferred_element_type=F32)
            if a == 2:
                acc[b] = product
            else:
                acc[b] = acc[b] + product
            return carry

        lax.fori_loop(0, 3, tap, 0)

    activate_main(2)

    @pl.when(has[1])
    def _():
        to_next.wait_recv()

    @pl.when(relay)
    def _():
        to_relay.start()

    @pl.when(has[1])
    def _():
        start_halo(1)

    wait_halo(2)
    activate_halo(2)
    load.wait()
    convolve(2)

    @pl.when(has[0])
    def _():
        to_skip.wait_recv()
        start_halo(0)

    @pl.when(has[1])
    def _():
        tab_next.wait_recv()
        activate_main(1)
        wait_halo(1)
        activate_halo(1)
        convolve(1)

    @pl.when(has[0])
    def _():
        tab_skip.wait_recv()
        activate_main(0)
        wait_halo(0)
        activate_halo(0)
        convolve(0)

    source = lat[...].astype(F32)
    rows = []
    for r in range(ROWS):
        own = labels[first + r]
        lines = pl.ds(r * WIDE, COLS)
        total = acc[1, lines, :]
        total = total + jnp.where(labels[first + r - 1] == own, acc[0, lines, :], 0.0)
        total = total + jnp.where(labels[first + r + 1] == own, acc[2, lines, :], 0.0)
        total = source[r * COLS : (r + 1) * COLS] + total + bias[...]
        rows.append(jnp.where(column < widths[first + r], total, 0.0))
    out[...] = jnp.concatenate(rows, axis=0).astype(BF16)

    @pl.when(next_frame)
    def _():
        to_next.wait_send()
        tab_next.wait_send()

    @pl.when(frame + 2 < FRAMES)
    def _():
        tab_skip.wait_send()

    @pl.when(skip_frame)
    def _():
        to_skip.wait_send()

    @pl.when(relay)
    def _():
        to_relay.wait_send()

    end_halo(2)

    @pl.when(has[1])
    def _():
        end_halo(1)

    @pl.when(has[0])
    def _():
        end_halo(0)


def attention_kernel(
    labels, widths, own, onehot_sum, onehot_sum_t, onehot_both, row_cells, inverse, member,
    member_t, gain, shift, triple_weight, triple_bias, output_weight, output_bias,
    result, result_top, result_bot,
    kv, qb, gat, st, tab, keys, queries, scores, sent, parts, rim, top, bot,
    stat_send, stat_recv, kv_send, kv_recv, q_send, q_recv, part_send, part_recv,
    halo_send, halo_recv,
):
    tile, frame, x, y, z = place()
    first = tile * ROWS + 1
    above = tile >= 1
    below = tile + 1 < TILES
    barrier = pltpu.get_barrier_semaphore()
    for k in range(1, 8):
        greet(barrier, tile_at(x, y + k // 2, z + k % 2), frame)
    for d in range(1, 4):
        greet(barrier, tile_at(x + d, y, z), frame)
    awaited = 10
    for there, step in ((above, -1), (below, 1)):

        @pl.when(there)
        def _():
            greet(barrier, tile + step, frame)

        awaited = awaited + there.astype(jnp.int32)
    pl.semaphore_wait(barrier, awaited)

    kv_copies = []
    for k in range(1, 8):
        peer = tile_at(x, y + k // 2, z + k % 2)
        kv_copies.append(
            remote(own, kv.at[k - 1], kv_send.at[k - 1], kv_recv.at[k - 1], peer, frame)
        )
    q_copies = []
    for d in range(1, 4):
        peer = tile_at(x + d, y, z)
        q_copies.append(remote(own, qb.at[d - 1], q_send.at[d - 1], q_recv.at[d - 1], peer, frame))
    for copy in kv_copies + q_copies:
        copy.start()

    source = own[...].astype(F32)
    gat[tile] = local_sums(source, labels, widths, first, member[...], member_t[...], st)
    gather_sums(gat, stat_send, stat_recv)
    mean, scale = combine_sums(
        gat, onehot_sum[...], onehot_sum_t[...], onehot_both[...], row_cells[...], inverse[...],
        member[...],
    )
    tab[0:8, :] = mean
    tab[8:16, :] = scale
    column = lax.broadcasted_iota(jnp.int32, (COLS, CH), 0)
    cell_column = lax.broadcasted_iota(jnp.int32, (COLS, LANES), 0)
    lane = lax.broadcasted_iota(jnp.int32, (COLS, LANES), 1)
    wide_lane = lax.broadcasted_iota(jnp.int32, (CELLS, LANES), 1)
    to_exponent = CH ** (-0.5) * math.log2(math.e)

    def normalise(block, block_tile):
        cells = block.astype(F32)
        rows = []
        for r in range(ROWS):
            at = block_tile * ROWS + 1 + r
            row_mean, row_scale = pick(tab, labels[at])
            part = cells[r * COLS : (r + 1) * COLS]
            normed = (part - row_mean) * row_scale * gain[...] + shift[...]
            rows.append(jnp.where(column < widths[at], normed, 0.0))
        return jnp.concatenate(rows, axis=0).astype(BF16)

    def put_query(slot, block, block_tile):
        normed = normalise(block, block_tile)
        plain = jnp.dot(normed, triple_weight[:, 0:CH], preferred_element_type=F32)
        plain = (plain + triple_bias[:, 0:CH]).astype(BF16)
        turned = lax.dot_general(
            plain, triple_weight[:, CH : 2 * CH], NT, preferred_element_type=F32
        )
        constant = jnp.sum(
            plain.astype(F32) * triple_bias[:, CH : 2 * CH], axis=1, keepdims=True
        )
        queries[slot, :, 0:CH] = (turned * to_exponent).astype(BF16)
        marks = []
        for r in range(ROWS):
            label = labels[block_tile * ROWS + 1 + r]
            marks.append(jnp.where(lane == label, 1.0, 0.0))
        marks = jnp.concatenate(marks, axis=0)
        marks = jnp.where(wide_lane == 4, constant * to_exponent, marks)
        queries[slot, :, CH:EXT] = marks.astype(BF16)

    def put_keys(slot, block, block_tile):
        lines = pl.ds(pl.multiple_of(slot * CELLS, 16), CELLS)
        keys[lines, 0:CH] = normalise(block, block_tile)
        marks = []
        for r in range(ROWS):
            at = block_tile * ROWS + 1 + r
            seen = (lane == labels[at]) & (cell_column < widths[at])
            mark = jnp.where(seen, 0.0, MASKED)
            marks.append(jnp.where(lane < 4, mark, jnp.where(lane == 4, 1.0, 0.0)))
        keys[lines, CH:EXT] = jnp.concatenate(marks, axis=0).astype(BF16)

    put_query(0, own[...], tile)
    put_keys(0, own[...], tile)
    for k in range(1, 8):
        kv_copies[k - 1].wait_recv()
    for d in range(1, 4):
        q_copies[d - 1].wait_recv()

    def each_query(d, carry):
        put_query(d, qb[d - 1], tile_at(x + 4 - d, y, z))
        return carry

    lax.fori_loop(1, 4, each_query, 0)

    def each_key(k, carry):
        put_keys(k, kv[k - 1], tile_at(x, y + 4 - lax.div(k, 2), z + lax.rem(k, 2)))
        return carry

    lax.fori_loop(1, 8, each_key, 0)

    def attend(d):
        slot = lax.rem(4 - d, 4)
        scores[...] = lax.dot_general(queries[slot], keys[...], NT, preferred_element_type=F32)
        held = scores[...]
        largest = jnp.max(held, axis=1, keepdims=True).astype(BF16).astype(F32)
        weights = jnp.exp2(held - largest).astype(BF16)
        mixed = jnp.dot(weights, keys[...], preferred_element_type=F32)
        sent[d, :, 0:CH] = mixed[:, 0:CH].astype(BF16)
        total = mixed[:, CH + 4 : CH + 5]
        high = total.astype(BF16).astype(F32)
        notes = jnp.where(wide_lane == 4, high, 0.0)
        notes = jnp.where(wide_lane == 5, largest, notes)
        notes = jnp.where(wide_lane == 6, total - high, notes)
        sent[d, :, CH:EXT] = notes.astype(BF16)

    def part_copy(d):
        return remote(
            sent.at[d], parts.at[d], part_send.at[d], part_recv.at[d], tile_at(x + d, y, z), frame
        )

    def each_part(n, carry):
        d = 3 - n
        attend(d)

        @pl.when(d > 0)
        def _():
            part_copy(d).start()

        return carry

    lax.fori_loop(0, 4, each_part, 0)
    for d in range(3, 0, -1):
        part_copy(d).wait_recv()

    def part(d, lanes):
        return (sent[0, :, lanes] if d == 0 else parts[d, :, lanes]).astype(F32)

    tails = [part(d, pl.ds(CH, LANES)) for d in range(4)]
    maxima = [tail[:, 5:6] for tail in tails]
    most = functools.reduce(jnp.maximum, maxima)
    factors = [jnp.exp2(m - most) for m in maxima]
    denominator = sum((t[:, 4:5] + t[:, 6:7]) * f for t, f in zip(tails, factors))
    numerator = sum(part(d, pl.ds(0, CH)) * factors[d] for d in range(4))
    averaged = (numerator / denominator).astype(BF16)
    mixed = jnp.dot(averaged, triple_weight[:, 2 * CH : 3 * CH], preferred_element_type=F32)
    mixed = (mixed + triple_bias[:, 2 * CH : 3 * CH]).astype(BF16)
    attended = jnp.dot(mixed, output_weight[...], preferred_element_type=F32)
    total = own[...].astype(F32) + attended + output_bias[...]
    rows = []
    for r in range(ROWS):
        rows.append(
            jnp.where(column < widths[first + r], total[r * COLS : (r + 1) * COLS], 0.0)
        )
    rim[...] = jnp.concatenate(rows, axis=0).astype(BF16)
    up = remote(rim.at[pl.ds(0, WIDE)], bot, halo_send.at[0], halo_recv.at[0], tile - 1, frame)
    down = remote(rim.at[pl.ds(LAST, WIDE)], top, halo_send.at[1], halo_recv.at[1], tile + 1, frame)

    @pl.when(above)
    def _():
        up.start()

    @pl.when(below)
    def _():
        down.start()

    result[...] = rim[...]
    for copy in kv_copies + q_copies:
        copy.wait_send()
    for d in range(3, 0, -1):
        part_copy(d).wait_send()

    @pl.when(below)
    def _():
        up.wait_recv()
        result_bot[...] = bot[...]
        down.wait_send()

    @pl.when(above)
    def _():
        down.wait_recv()
        result_top[...] = top[...]
        up.wait_send()

    @pl.when(jnp.logical_not(below))
    def _():
        result_bot[...] = jnp.zeros((WIDE, CH), BF16)

    @pl.when(jnp.logical_not(above))
    def _():
        result_top[...] = jnp.zeros((WIDE, CH), BF16)


def upsample_kernel(labels, widths, main, top, bot, weight, bias, out, taps, ends, low, high):
    first = lax.axis_index("tile") * ROWS + 1

    def product(k, carry):
        taps[k, :, 0:OUT] = jnp.dot(main[...], weight[k], preferred_element_type=F32)
        return carry

    lax.fori_loop(0, 9, product, 0)
    for e in range(3):
        ends[e, :, 0:OUT] = jnp.dot(top[...], weight[e], preferred_element_type=F32)
        ends[3 + e, :, 0:OUT] = jnp.dot(bot[...], weight[6 + e], preferred_element_type=F32)
    column = lax.broadcasted_iota(jnp.int32, (COLS, 2 * LANES), 0)
    for r in range(ROWS):
        own = labels[first + r]
        lines = pl.ds(r * COLS, COLS)
        for p in range(2):
            joined = []
            other = r - 1 if p == 0 else r + 1
            alike = labels[first + other] == own
            outer = 0 if p == 0 else 2
            for e in range(3):
                if other < 0:
                    far = ends[e, WIDE - COLS :, :]
                elif other == ROWS:
                    far = ends[3 + e, :COLS, :]
                else:
                    far = taps[outer * 3 + e, pl.ds(other * COLS, COLS), :]
                near = taps[3 + e, lines, :] + taps[(2 - outer) * 3 + e, lines, :]
                joined.append(near + jnp.where(alike, far, 0.0))
            before = jnp.where(column == 0, 0.0, pltpu.roll(joined[0], 1, 0))
            after = jnp.where(column == COLS - 1, 0.0, pltpu.roll(joined[2], COLS - 1, 0))
            valid = column < widths[first + r]
            left = before + joined[1] + joined[2] + bias[...]
            right = joined[0] + joined[1] + after + bias[...]
            left = jnp.where(valid, left, 0.0)
            right = jnp.where(valid, right, 0.0)
            for half, lanes in ((low, slice(0, LANES)), (high, slice(LANES, 2 * LANES))):
                half[pl.ds(0, COLS, stride=2), :] = left[:, lanes]
                half[pl.ds(1, COLS, stride=2), :] = right[:, lanes]
            out[2 * r + p, :, 0:LANES] = low[...].astype(BF16)
            out[2 * r + p, :, LANES:OUT] = high[:, 0 : OUT - LANES].astype(BF16)


def shards(
    latents,
    row_video,
    video_cols,
    first_gain,
    first_shift,
    conv_weight,
    conv_bias,
    second_gain,
    second_shift,
    triple_weight,
    triple_bias,
    output_weight,
    output_bias,
    upsample_weight,
    upsample_bias,
):
    videos = video_cols.shape[0]
    matches = row_video[:, None] == jnp.arange(videos, dtype=jnp.int32)[None, :]
    canvas_widths = jnp.sum(jnp.where(matches, video_cols[None, :], 0), axis=1)
    labels = jnp.pad(row_video, 1, constant_values=-1)
    widths = jnp.pad(canvas_widths, 1)
    lines = jnp.tile(row_video.reshape(TILES, 1, ROWS), (1, 2, 1)).reshape(TILES * 8)
    numbers = jnp.arange(8, dtype=jnp.int32)
    both = lines[None, :] == numbers[:, None]
    upper = (jnp.arange(TILES * 8) % 8 < ROWS)[None, :]
    onehot_both = both.astype(F32)
    onehot_sum = (both & upper).astype(F32)
    onehot_sum_t = ((lines[:, None] == numbers[None, :]) & upper.T).astype(F32)
    per_group = CH // GROUPS
    line_widths = jnp.tile(canvas_widths.reshape(TILES, 1, ROWS), (1, 2, 1)).reshape(-1, 1)
    row_cells = line_widths.astype(F32) * per_group
    counts = jnp.sum(jnp.where(matches, canvas_widths[:, None], 0), axis=0) * per_group
    inverse = jnp.pad(1.0 / counts.astype(F32), (0, 8 - videos))[:, None]
    member = (
        np.arange(LANES)[:, None] == np.arange(CH)[None, :] // per_group
    ).astype(np.float32)
    tables = (onehot_sum, onehot_sum_t, onehot_both, row_cells, inverse, member, member.T)

    def line(vector):
        return vector.reshape(1, -1)

    smem = pl.BlockSpec(memory_space=pltpu.SMEM)
    vmem = pl.BlockSpec(memory_space=pltpu.VMEM)
    anywhere = pl.BlockSpec(memory_space=pl.ANY)
    dma = pltpu.SemaphoreType.DMA
    after_conv = pl.pallas_call(
        front_kernel,
        out_shape=jax.ShapeDtypeStruct((CELLS, CH), BF16),
        in_specs=[smem, smem] + [vmem] * 10 + [anywhere, vmem],
        out_specs=vmem,
        scratch_shapes=[
            pltpu.VMEM((2, CELLS, CH), BF16),
            pltpu.VMEM((3, WIDE, CH), BF16),
            pltpu.VMEM((3, WIDE, CH), BF16),
            pltpu.VMEM((TILES, 8, LANES), F32),
            pltpu.VMEM((8, CH), F32),
            pltpu.VMEM((3, 16, CH), F32),
            pltpu.VMEM((3, 6 * WIDE, 3 * CH), BF16),
            pltpu.VMEM((9, 3 * CH, CH), BF16),
            pltpu.VMEM((3, PADDED, CH), F32),
            dma((7,)),
            dma((7,)),
            dma((3,)),
            dma((2,)),
            dma((3, 2)),
            dma((3, 2)),
            dma((2,)),
            dma((2,)),
            dma,
        ],
        compiler_params=pltpu.CompilerParams(
            collective_id=0, has_side_effects=True, vmem_limit_bytes=48 * 2**20
        ),
        name="norm_conv",
    )(
        labels, widths, latents.reshape(CELLS, CH), *tables, line(first_gain), line(first_shift),
        conv_weight.reshape(9, 3 * CH, CH), line(conv_bias),
    )
    edge = jax.ShapeDtypeStruct((WIDE, CH), BF16)
    rims = pl.pallas_call(
        attention_kernel,
        out_shape=[jax.ShapeDtypeStruct((CELLS, CH), BF16), edge, edge],
        in_specs=[smem, smem] + [vmem] * 14,
        out_specs=[vmem] * 3,
        scratch_shapes=[
            pltpu.VMEM((7, CELLS, CH), BF16),
            pltpu.VMEM((3, CELLS, CH), BF16),
            pltpu.VMEM((TILES, 8, LANES), F32),
            pltpu.VMEM((8, CH), F32),
            pltpu.VMEM((16, CH), F32),
            pltpu.VMEM((KEYS, EXT), BF16),
            pltpu.VMEM((4, CELLS, EXT), BF16),
            pltpu.VMEM((CELLS, KEYS), F32),
            pltpu.VMEM((4, CELLS, EXT), BF16),
            pltpu.VMEM((4, CELLS, EXT), BF16),
            pltpu.VMEM((CELLS, CH), BF16),
            pltpu.VMEM((WIDE, CH), BF16),
            pltpu.VMEM((WIDE, CH), BF16),
            dma((7,)),
            dma((7,)),
            dma((7,)),
            dma((7,)),
            dma((3,)),
            dma((3,)),
            dma((4,)),
            dma((4,)),
            dma((2,)),
            dma((2,)),
        ],
        compiler_params=pltpu.CompilerParams(
            collective_id=1, has_side_effects=True, vmem_limit_bytes=48 * 2**20
        ),
        name="attention",
    )(
        labels, widths, after_conv, *tables, line(second_gain), line(second_shift), triple_weight,
        line(triple_bias), output_weight, line(output_bias),
    )
    wide_bias = jnp.pad(line(upsample_bias), ((0, 0), (0, 2 * LANES - OUT)))
    decoded = pl.pallas_call(
        upsample_kernel,
        out_shape=jax.ShapeDtypeStruct((2 * ROWS, 2 * COLS, OUT), BF16),
        in_specs=[smem, smem] + [vmem] * 5,
        out_specs=vmem,
        scratch_shapes=[
            pltpu.VMEM((9, CELLS, 2 * LANES), F32),
            pltpu.VMEM((6, WIDE, 2 * LANES), F32),
            pltpu.VMEM((2 * COLS, LANES), F32),
            pltpu.VMEM((2 * COLS, LANES), F32),
        ],
        compiler_params=pltpu.CompilerParams(vmem_limit_bytes=32 * 2**20),
        name="upsample",
    )(labels, widths, *rims, upsample_weight.reshape(9, CH, OUT), wide_bias)
    return decoded.reshape(2 * ROWS, 1, 2 * COLS, OUT)


def solution(mesh):
    in_specs = (P("tile", "frame", None, None),) + (P(),) * 14
    out_specs = P("tile", "frame", None, None)
    return jax.shard_map(shards, mesh=mesh, in_specs=in_specs, out_specs=out_specs, check_vma=False)
```

time: 928 us -> 144 us (0.16)
  waiting for transfers between devices: 457 us -> 0 us
  blocking collectives: 306 us -> 0 us
  Pallas kernels: 0 us -> 128 us
  local copies, waits for them, and re-layouts: 48.7 us -> 14.1 us
  matrix products: 31.5 us -> 0 us
  starting transfers between devices: 27.4 us -> 0 us
  loops' own time: 21 us -> 0 us
  other arithmetic: 20.3 us -> 1.68 us
  between operations: 14 us -> 0.13 us
    all_gather x1 -> x0, waiting for transfers between devices: 447 us -> none  [shards(): lax.all_gather(triple[..., channels:], 'tile', axis=0, tiled=True)]
    psum x4 -> x0, blocking collectives: 306 us -> none  [the longest x2 157 us: group_norm(): variance = lax.psum(partial_spread, 'tile') / counts]
    pallas_call x0 -> x3, Pallas kernels: none -> 128 us  [the longest x1 75.8 us: shards(): pl.pallas_call(attention_kernel, out_shape=[jax.ShapeDtypeStruct((CELLS,...]
    dot_general x44 -> x0, matrix products: 31.5 us -> none  [the longest x7 8.1 us: update(): jnp.einsum('rfwk,fkc->rfwc', weights.astype(jnp.bfloat16), value_flat, pr...]
    slice x33 -> x0, local copies, waits for them, and re-layouts: 29.7 us -> none  [the longest x7 13.7 us: split_pairs(): return (block[..., :channels], block[..., channels:])]
    ppermute x6 -> x0, starting transfers between devices: 27.4 us -> none  [the longest x2 12.5 us: padded_2(): after = lax.ppermute(leading, axis, down)]
    another operation x9 -> x0, loops' own time: 21 us -> none  [the longest x1 20.3 us: shards(): folded = lax.fori_loop(0, piece_rows // step_rows, advance, initial)]
    ppermute x6 -> x0, waiting for transfers between devices: 10.1 us -> none  [the longest x2 8.56 us: shifted(): return lax.ppermute(shard, axis, pairs)]
  transfers between devices with their start and end apart: 7 -> 0, of which waited for: 5 -> 0; matrix products, arithmetic and copies ran while one was open for 1% -> 0% of each run, Pallas kernels for 0% -> 0%
where the time goes in v2:
time: 144 us
  Pallas kernels  128 us (89%)
  local copies, waits for them, and re-layouts  14.1 us (10%)
  other arithmetic  1.68 us (1%)
    pallas_call x1, Pallas kernels, shards(): pl.pallas_call(attention_kernel, out_shape=[jax.ShapeDtypeStruct((CELLS,...  75.8 us
    pallas_call x1, Pallas kernels, shards(): pl.pallas_call(front_kernel, out_shape=jax.ShapeDtypeStruct((CELLS, CH),...  48.1 us
    unnamed x11, local copies, waits for them, and re-layouts  5.35 us
    reshape x7, local copies, waits for them, and re-layouts, line(): return vector.reshape(1, -1)  4.8 us
    pallas_call x1, Pallas kernels, shards(): pl.pallas_call(upsample_kernel, out_shape=jax.ShapeDtypeStruct((2 * ROWS,...  4.21 us

profile of v2, /device:TPU:66, one launch (start us, length us, event | category | flops | bytes accessed | tf_op | source)
XLA Modules:
  0.0 144.0 jit_solution(10345840558960401225)
XLA Ops:
  0.0 0.8 select_reduce_fusion.1
  0.8 0.8 select_reduce_fusion
  1.6 0.1 pad.16.widths
  1.6 0.7 pad.15.labels
  2.4 0.7 pad.18.bias
  3.0 0.7 reshape.97.gain
  3.7 0.7 reshape.98.shift
  4.4 0.7 reshape.100.bias
  5.1 0.7 reshape.101.gain
  5.8 0.7 reshape.102.shift
  6.5 0.7 reshape.104.output_bias
  7.1 0.1 copy.29.inverse
  7.2 0.7 reshape.103.triple_bias
  7.9 0.1 mul.15
  8.1 0.8 tile.14
  8.8 0.1 tile.16
  9.0 0.1 mul.18.row_cells
  9.1 0.1 fusion.1.onehot_sum_t
  9.2 0.0 copy-start.1
  9.2 0.9 copy-done.1
  10.1 0.0 copy-start.2
  10.2 0.9 copy-done.2
  11.1 0.0 copy-start.3
  11.1 1.0 copy-done.3
  12.0 0.0 copy-start
  12.0 0.0 copy-start.4
  12.1 48.1 %norm_conv.1.own = bf16[416,384]{1,0:T(8,128)(2,1)S(1)} custom-call(s32[130]{0:T(256)S(1)} %pad.15.labels, s32[130]{0:T(256)S(1)} %pad.16.widths, bf16[416,384]{1,0:T(8,128)(2,1)S(1)} %bitcast.13, f32[8,256]{1,0:T(8,128)S(1)} %get-tuple-element.12.onehot_sum, f32[256,8]{1,0:T(8,128)S(1)} %fusion.1.onehot_sum_t, f32[8,256]{1,0:T(8,128)S(1)} %get-tuple-element.11.onehot_both, ...), custom_call_target="tpu_custom_call" | custom-call | tf_op jit(solution)/shard_map/norm_conv/pallas_call | solution.py:679
  60.1 0.0 copy-done
  60.2 0.0 copy-done.4
  60.2 75.8 %attention.1 = (bf16[416,384]{1,0:T(8,128)(2,1)S(1)}, bf16[112,384]{1,0:T(8,128)(2,1)S(1)}, bf16[112,384]{1,0:T(8,128)(2,1)S(1)}) custom-call(s32[130]{0:T(256)S(1)} %pad.15.labels, s32[130]{0:T(256)S(1)} %pad.16.widths, bf16[416,384]{1,0:T(8,128)(2,1)S(1)} %norm_conv.1.own, f32[8,256]{1,0:T(8,128)S(1)} %get-tuple-element.12.onehot_sum, ...), custom_call_target="tpu_custom_call" | custom-call | tf_op jit(solution)/shard_map/attention/pallas_call | solution.py:713
  136.0 2.5 %copy.32 = bf16[3,3,384,192]{3,2,1,0:T(8,128)(2,1)S(1)} copy(bf16[3,3,384,192]{2,3,1,0:T(8,128)(2,1)} %param.30) | data formatting | bytes 2654208 | tf_op args[13]
  138.5 4.2 %upsample.1 = bf16[8,208,192]{2,1,0:T(8,128)(2,1)S(1)} custom-call(s32[130]{0:T(256)S(1)} %pad.15.labels, s32[130]{0:T(256)S(1)} %pad.16.widths, bf16[416,384]{1,0:T(8,128)(2,1)S(1)} %get-tuple-element.8.main, bf16[112,384]{1,0:T(8,128)(2,1)S(1)} %get-tuple-element.9.top, bf16[112,384]{1,0:T(8,128)(2,1)S(1)} %get-tuple-element.10.bot, ...), custom_call_target="tpu_custom_call" | custom-call | tf_op jit(solution)/shard_map/upsample/pallas_call | solution.py:752
  142.7 1.3 copy.33
  (7 shorter events, 0.1 us)
Async XLA Ops:
  9.2 0.9 copy-start.1
  10.1 0.9 copy-start.2
  11.1 1.0 copy-start.3
  12.0 48.1 %copy-start = (bf16[384,1152]{1,0:T(8,128)(2,1)S(1)}, bf16[384,1152]{1,0:T(8,128)(2,1)}, u32[]{:S(2)}) copy-start(bf16[384,1152]{1,0:T(8,128)(2,1)} %triple_weight.1) | copy-start | bytes 2654212
  12.0 48.1 %copy-start.4 = (bf16[384,384]{1,0:T(8,128)(2,1)S(1)}, bf16[384,384]{1,0:T(8,128)(2,1)}, u32[]{:S(2)}) copy-start(bf16[384,384]{1,0:T(8,128)(2,1)} %output_weight.1) | copy-start | bytes 884740

commit v3 on v2

v3 whole, which is shorter than its diff:
```python
import functools
import math

import jax
import jax.numpy as jnp
from jax import lax
from jax.experimental import pallas as pl
from jax.experimental.pallas import tpu as pltpu
from jax.sharding import PartitionSpec as P

GROUPS = 32
EPSILON = 1e-05
MASKED = -1e30
HIGHEST = lax.Precision.HIGHEST
MESH = pl.DeviceIdType.MESH
F32 = jnp.float32
BF16 = jnp.bfloat16
CH = 384
OUT = 192
ROWS = 4
COLS = 104
WIDE = 112
CELLS = ROWS * COLS
PADDED = ROWS * WIDE
LAST = CELLS - WIDE
LANES = 128
EXT = CH + LANES
TILES = 32
FRAMES = 8
KEYS = 8 * CELLS
NT = (((1,), (1,)), ((), ()))


def remote(src, dst, send_sem, recv_sem, tile, frame):
    return pltpu.make_async_remote_copy(
        src_ref=src,
        dst_ref=dst,
        send_sem=send_sem,
        recv_sem=recv_sem,
        device_id={"tile": tile, "frame": frame},
        device_id_type=MESH,
    )


def place():
    tile = lax.axis_index("tile")
    frame = lax.axis_index("frame")
    x = lax.div(tile, 8)
    y = lax.rem(lax.div(tile, 2), 4)
    z = lax.rem(tile, 2)
    return tile, frame, x, y, z


def tile_at(x, y, z):
    return lax.rem(x, 4) * 8 + lax.rem(y, 4) * 2 + lax.rem(z, 2)


def greet(barrier, tile, frame):
    pl.semaphore_signal(
        barrier, inc=1, device_id={"tile": tile, "frame": frame}, device_id_type=MESH
    )


def exact(a, b):
    return jnp.dot(a, b, precision=HIGHEST, preferred_element_type=F32)


def line_of(vector, part=None):
    held = vector[...] if part is None else vector[pl.ds(part * CH, CH)]
    return held.reshape(1, held.shape[0])


def pick(table, label):
    rows = lax.broadcasted_iota(jnp.int32, (8, CH), 0)
    chosen = rows == label
    mean = jnp.sum(jnp.where(chosen, table[0:8, :], 0.0), axis=0, keepdims=True)
    scale = jnp.sum(jnp.where(chosen, table[8:16, :], 0.0), axis=0, keepdims=True)
    return mean, scale


def members():
    per_group = CH // GROUPS
    start = lax.broadcasted_iota(jnp.int32, (LANES, CH), 0) * per_group
    channel = lax.broadcasted_iota(jnp.int32, (LANES, CH), 1)
    across = jnp.where((channel >= start) & (channel < start + per_group), 1.0, 0.0)
    start = lax.broadcasted_iota(jnp.int32, (CH, LANES), 1) * per_group
    channel = lax.broadcasted_iota(jnp.int32, (CH, LANES), 0)
    down = jnp.where((channel >= start) & (channel < start + per_group), 1.0, 0.0)
    return across, down


def local_sums(values, width_of, first, st):
    member, member_t = members()
    column = lax.broadcasted_iota(jnp.int32, (COLS, CH), 0)
    line = lax.broadcasted_iota(jnp.int32, (8, 1), 0)
    per_row = jnp.ones((8, 1), F32)
    for r in range(ROWS):
        width = width_of(first + r)
        mask = column < width
        cells = values[r * COLS : (r + 1) * COLS]
        total = jnp.sum(jnp.where(mask, cells, 0.0), axis=0, keepdims=True)
        mean = total / width.astype(F32)
        apart = jnp.where(mask, cells - mean, 0.0)
        st[r : r + 1, :] = total
        st[ROWS + r : ROWS + r + 1, :] = jnp.sum(apart * apart, axis=0, keepdims=True)
        per_row = jnp.where((line == r) | (line == ROWS + r), width.astype(F32), per_row)
    upper = line < ROWS
    held = st[...]
    grouped = exact(held, member_t)
    group_mean = exact(jnp.where(upper, grouped / (per_row * (CH // GROUPS)), 0.0), member)
    spread = jnp.where(upper, held / per_row - group_mean, 0.0)
    extra = exact(per_row * spread * spread, member_t)
    lower = pltpu.roll(extra, ROWS, 0)
    return jnp.where(upper, grouped, grouped + lower)


def combine_sums(gat, onehot, row_cells):
    member, _ = members()
    held = gat.reshape(TILES * 8, LANES)
    upper = lax.rem(lax.broadcasted_iota(jnp.int32, (TILES * 8, LANES), 0), 8) < ROWS
    by_video = jnp.transpose(onehot)[0:8]
    counts = exact(by_video, jnp.where(upper, row_cells, 0.0))
    inverse = jnp.where(counts > 0.0, 1.0 / counts, 0.0)
    mean = exact(by_video, jnp.where(upper, held, 0.0)) * inverse
    mean_rows = exact(onehot[:, 0:8], mean)
    off = held / row_cells - mean_rows
    spread = jnp.where(upper, row_cells * off * off, held)
    variance = exact(by_video, spread) * inverse
    scale = lax.rsqrt(variance + EPSILON)
    return exact(mean, member), exact(scale, member)


def whole_kernel(
    videos, cols, lat_hbm, first_gain, first_shift, conv_hbm, conv_bias, second_gain, second_shift,
    triple_weight, triple_bias, output_weight, output_bias, up_weight, up_bias, out,
    lat, main, top, bot, gat, onehot, row_cells, st, tabs, hid, weight, acc,
    own, kv, qb, tab, keys, queries, scores, sent, parts, rim, rim_top, rim_bot,
    taps, ends, low, high, wide_bias,
    stat_send, stat_recv, main_send, main_recv, halo_send, halo_recv, tab_send, tab_recv,
    load_sem, kv_send, kv_recv, q_send, q_recv, part_send, part_recv, rim_send, rim_recv,
):
    tile, frame, x, y, z = place()
    first = tile * ROWS
    load_lat = pltpu.make_async_copy(lat_hbm, lat, load_sem.at[0])
    load_lat.start()
    load = pltpu.make_async_copy(conv_hbm, weight, load_sem.at[1])
    load.start()

    def label_of(row):
        inside = (row >= 0) & (row < TILES * ROWS)
        return jnp.where(inside, videos[jnp.clip(row, 0, TILES * ROWS - 1)], -1)

    def width_of(row):
        inside = (row >= 0) & (row < TILES * ROWS)
        return jnp.where(inside, cols[videos[jnp.clip(row, 0, TILES * ROWS - 1)]], 0)

    barrier = pltpu.get_barrier_semaphore()

    def greet_tile(d, carry):
        greet(barrier, lax.rem(tile + d, TILES), frame)
        return carry

    lax.fori_loop(1, TILES, greet_tile, 0)
    awaited = TILES - 1
    for step in (-2, -1, 1, 2):
        there = (frame + step >= 0) & (frame + step < FRAMES)

        @pl.when(there)
        def _():
            greet(barrier, tile, frame + step)

        awaited = awaited + there.astype(jnp.int32)

    slot_line = lax.rem(lax.broadcasted_iota(jnp.int32, (8, LANES), 0), ROWS)
    slot_lane = lax.broadcasted_iota(jnp.int32, (8, LANES), 1)

    def fill(t, carry):
        label = jnp.full((8, LANES), -1, jnp.int32)
        width = jnp.zeros((8, LANES), jnp.int32)
        for r in range(ROWS):
            number = videos[t * ROWS + r]
            label = jnp.where(slot_line == r, number, label)
            width = jnp.where(slot_line == r, cols[number], width)
        lines = pl.ds(pl.multiple_of(t * 8, 8), 8)
        onehot[lines, :] = jnp.where(label == slot_lane, 1.0, 0.0)
        row_cells[lines, :] = width.astype(F32) * (CH // GROUPS)
        return carry

    lax.fori_loop(0, TILES, fill, 0)
    wide_bias[...] = jnp.zeros((1, 2 * LANES), F32)
    wide_bias[:, 0:OUT] = line_of(up_bias)
    load_lat.wait()
    source = lat[...].astype(F32)
    gat[0, tile] = local_sums(source, width_of, first, st)
    pl.semaphore_wait(barrier, awaited)

    def sum_copy(which, d):
        peer = lax.rem(tile + d, TILES)
        return remote(
            gat.at[which, tile], gat.at[which, tile], stat_send.at[which], stat_recv.at[which],
            peer, frame,
        )

    def send_sums(which):
        def one(d, carry):
            sum_copy(which, d).start()
            return carry

        lax.fori_loop(1, TILES, one, 0)

    def all_sums(which):
        others = pl.ds(0, TILES - 1)
        return remote(
            gat.at[which, others], gat.at[which, others], stat_send.at[which],
            stat_recv.at[which], lax.rem(tile + 1, TILES), frame,
        )

    send_sums(0)

    even = lax.rem(frame, 2) == 0
    next_frame = frame + 1 < FRAMES
    skip_frame = even & (frame + 2 < FRAMES)
    relay = even & (frame >= 2)
    has = {1: frame >= 1, 0: frame >= 2}
    above = tile >= 1
    below = tile + 1 < TILES

    to_next = remote(lat, main.at[1], main_send.at[1], main_recv.at[1], tile, frame + 1)
    to_skip = remote(lat, main.at[0], main_send.at[0], main_recv.at[0], tile, frame + 2)
    to_relay = remote(main.at[1], main.at[0], main_send.at[2], main_recv.at[0], tile, frame + 1)

    def halo(a):
        src = lat if a == 2 else main.at[a]
        up = remote(
            src.at[pl.ds(0, WIDE)], bot.at[a], halo_send.at[a, 0], halo_recv.at[a, 0],
            tile - 1, frame,
        )
        down = remote(
            src.at[pl.ds(LAST, WIDE)], top.at[a], halo_send.at[a, 1], halo_recv.at[a, 1],
            tile + 1, frame,
        )
        return up, down

    def start_halo(a):
        up, down = halo(a)

        @pl.when(above)
        def _():
            up.start()

        @pl.when(below)
        def _():
            down.start()

    def wait_halo(a):
        up, down = halo(a)

        @pl.when(below)
        def _():
            up.wait_recv()

        @pl.when(above)
        def _():
            down.wait_recv()

    def end_halo(a):
        up, down = halo(a)

        @pl.when(above)
        def _():
            up.wait_send()

        @pl.when(below)
        def _():
            down.wait_send()

    @pl.when(next_frame)
    def _():
        to_next.start()

    start_halo(2)

    all_sums(0).wait_recv()

    @pl.when(skip_frame)
    def _():
        to_skip.start()

    mean, scale = combine_sums(gat[0], onehot[...], row_cells[...])
    tabs[2, 0:8, :] = mean
    tabs[2, 8:16, :] = scale
    tab_next = remote(tabs.at[2], tabs.at[1], tab_send.at[1], tab_recv.at[1], tile, frame + 1)
    tab_skip = remote(tabs.at[2], tabs.at[0], tab_send.at[0], tab_recv.at[0], tile, frame + 2)

    @pl.when(next_frame)
    def _():
        tab_next.start()

    @pl.when(frame + 2 < FRAMES)
    def _():
        tab_skip.start()

    column = lax.broadcasted_iota(jnp.int32, (COLS, CH), 0)

    def activate(a, row, cells):
        label = label_of(first - 1 + row)
        width = width_of(first - 1 + row)
        row_mean, row_scale = pick(tabs[a], label)
        normed = (cells - row_mean) * row_scale * line_of(first_gain) + line_of(first_shift)
        hidden = normed / (1.0 + jnp.exp(-normed))
        hidden = jnp.where(column < width, hidden, 0.0)
        hidden = jnp.concatenate([hidden, jnp.zeros((WIDE - COLS, CH), F32)], axis=0)
        lines = pl.ds(row * WIDE, WIDE)
        hid[a, lines, 0:CH] = pltpu.roll(hidden, 1, 0).astype(BF16)
        hid[a, lines, CH : 2 * CH] = hidden.astype(BF16)
        hid[a, lines, 2 * CH : 3 * CH] = pltpu.roll(hidden, WIDE - 1, 0).astype(BF16)

    def activate_main(a):
        cells = lat[...].astype(F32) if a == 2 else main[a].astype(F32)
        for r in range(ROWS):
            activate(a, r + 1, cells[r * COLS : (r + 1) * COLS])

    def activate_halo(a):
        activate(a, 0, top[a].astype(F32)[WIDE - COLS :])
        activate(a, ROWS + 1, bot[a].astype(F32)[:COLS])

    def convolve(a):
        def tap(b, carry):
            lines = pl.ds(pl.multiple_of(b * WIDE, 16), PADDED)
            product = jnp.dot(hid[a, lines, :], weight[a * 3 + b], preferred_element_type=F32)
            if a == 2:
                acc[b] = product
            else:
                acc[b] = acc[b] + product
            return carry

        lax.fori_loop(0, 3, tap, 0)

    activate_main(2)
    wait_halo(2)
    activate_halo(2)
    load.wait()
    convolve(2)

    @pl.when(has[1])
    def _():
        to_next.wait_recv()

    @pl.when(relay)
    def _():
        to_relay.start()

    @pl.when(has[1])
    def _():
        start_halo(1)
        tab_next.wait_recv()
        activate_main(1)

    @pl.when(has[0])
    def _():
        to_skip.wait_recv()
        start_halo(0)

    @pl.when(has[1])
    def _():
        wait_halo(1)
        activate_halo(1)
        convolve(1)

    @pl.when(has[0])
    def _():
        tab_skip.wait_recv()
        activate_main(0)
        wait_halo(0)
        activate_halo(0)
        convolve(0)

    source = lat[...].astype(F32)
    rows = []
    for r in range(ROWS):
        label = label_of(first + r)
        lines = pl.ds(r * WIDE, COLS)
        total = acc[1, lines, :]
        total = total + jnp.where(label_of(first + r - 1) == label, acc[0, lines, :], 0.0)
        total = total + jnp.where(label_of(first + r + 1) == label, acc[2, lines, :], 0.0)
        total = source[r * COLS : (r + 1) * COLS] + total + line_of(conv_bias)
        rows.append(jnp.where(column < width_of(first + r), total, 0.0))
    own[...] = jnp.concatenate(rows, axis=0).astype(BF16)

    source = own[...].astype(F32)
    gat[1, tile] = local_sums(source, width_of, first, st)
    send_sums(1)

    half = CELLS // 2
    upper_half, lower_half = pl.ds(0, half), pl.ds(half, half)
    ahead, behind, across = tile_at(x, y + 1, z), tile_at(x, y + 3, z), tile_at(x, y, z + 1)

    def pass_on(k, src, slot, peer, lines=None):
        dst = kv.at[slot]
        if lines is not None:
            src, dst = src.at[lines], dst.at[lines]
        return remote(src, dst, kv_send.at[k], kv_recv.at[k], peer, frame)

    kv_across = pass_on(0, own, 4, across)
    kv_copies = [kv_across]
    relays = []
    for zz in range(2):
        base = own if zz == 0 else kv.at[4]
        near = (pass_on(1 + 4 * zz, base, zz * 4 + 1, ahead),
                pass_on(2 + 4 * zz, base, zz * 4 + 3, behind))
        far = (pass_on(3 + 4 * zz, kv.at[zz * 4 + 1], zz * 4 + 2, ahead, upper_half),
               pass_on(4 + 4 * zz, kv.at[zz * 4 + 3], zz * 4 + 2, behind, lower_half))
        relays.append((near, far))
        kv_copies += list(near) + list(far)
    q_copies = []
    for d in range(1, 4):
        peer = tile_at(x + d, y, z)
        q_copies.append(remote(own, qb.at[d - 1], q_send.at[d - 1], q_recv.at[d - 1], peer, frame))
    kv_across.start()
    for copy in relays[0][0]:
        copy.start()
    for copy in q_copies:
        copy.start()
    kv_across.wait_recv()
    for copy in relays[1][0]:
        copy.start()
    all_sums(1).wait_recv()
    mean, scale = combine_sums(gat[1], onehot[...], row_cells[...])
    tab[0:8, :] = mean
    tab[8:16, :] = scale
    column = lax.broadcasted_iota(jnp.int32, (COLS, CH), 0)
    cell_column = lax.broadcasted_iota(jnp.int32, (COLS, LANES), 0)
    lane = lax.broadcasted_iota(jnp.int32, (COLS, LANES), 1)
    wide_lane = lax.broadcasted_iota(jnp.int32, (CELLS, LANES), 1)
    to_exponent = CH ** (-0.5) * math.log2(math.e)

    def normalise(block, block_tile):
        cells = block.astype(F32)
        rows = []
        for r in range(ROWS):
            at = block_tile * ROWS + r
            row_mean, row_scale = pick(tab, label_of(at))
            part = cells[r * COLS : (r + 1) * COLS]
            normed = (part - row_mean) * row_scale * line_of(second_gain) + line_of(second_shift)
            rows.append(jnp.where(column < width_of(at), normed, 0.0))
        return jnp.concatenate(rows, axis=0).astype(BF16)

    def put_query(slot, block, block_tile):
        normed = normalise(block, block_tile)
        plain = jnp.dot(normed, triple_weight[:, 0:CH], preferred_element_type=F32)
        plain = (plain + line_of(triple_bias, 0)).astype(BF16)
        turned = lax.dot_general(
            plain, triple_weight[:, CH : 2 * CH], NT, preferred_element_type=F32
        )
        constant = jnp.sum(
            plain.astype(F32) * line_of(triple_bias, 1), axis=1, keepdims=True
        )
        queries[slot, :, 0:CH] = (turned * to_exponent).astype(BF16)
        marks = []
        for r in range(ROWS):
            label = label_of(block_tile * ROWS + r)
            marks.append(jnp.where(lane == label, 1.0, 0.0))
        marks = jnp.concatenate(marks, axis=0)
        marks = jnp.where(wide_lane == 4, constant * to_exponent, marks)
        queries[slot, :, CH:EXT] = marks.astype(BF16)

    def put_keys(slot, block, block_tile):
        lines = pl.ds(pl.multiple_of(slot * CELLS, 16), CELLS)
        keys[lines, 0:CH] = normalise(block, block_tile)
        marks = []
        for r in range(ROWS):
            at = block_tile * ROWS + r
            seen = (lane == label_of(at)) & (cell_column < width_of(at))
            mark = jnp.where(seen, 0.0, MASKED)
            marks.append(jnp.where(lane < 4, mark, jnp.where(lane == 4, 1.0, 0.0)))
        keys[lines, CH:EXT] = jnp.concatenate(marks, axis=0).astype(BF16)

    def key_tile(slot):
        return tile_at(x, y + 4 - lax.rem(slot, 4), z + lax.div(slot, 4))

    put_query(0, own[...], tile)
    put_keys(0, own[...], tile)
    for copy in relays[0][0]:
        copy.wait_recv()
    for copy in relays[0][1]:
        copy.start()
    put_keys(4, kv[4], across)
    for d in range(1, 4):
        q_copies[d - 1].wait_recv()

    def each_query(d, carry):
        put_query(d, qb[d - 1], tile_at(x + 4 - d, y, z))
        return carry

    lax.fori_loop(1, 4, each_query, 0)

    def put_pair(low_slot):
        def each_key(n, carry):
            slot = low_slot + 2 * n
            put_keys(slot, kv[slot], key_tile(slot))
            return carry

        lax.fori_loop(0, 2, each_key, 0)

    put_pair(1)
    for copy in relays[1][0]:
        copy.wait_recv()
    for copy in relays[1][1]:
        copy.start()
    put_pair(5)
    for zz in range(2):
        for copy in relays[zz][1]:
            copy.wait_recv()
        put_keys(zz * 4 + 2, kv[zz * 4 + 2], key_tile(jnp.int32(zz * 4 + 2)))

    def attend(d):
        slot = lax.rem(4 - d, 4)
        scores[...] = lax.dot_general(queries[slot], keys[...], NT, preferred_element_type=F32)
        held = scores[...]
        largest = jnp.max(held, axis=1, keepdims=True).astype(BF16).astype(F32)
        weights = jnp.exp2(held - largest).astype(BF16)
        mixed = jnp.dot(weights, keys[...], preferred_element_type=F32)
        sent[d, :, 0:CH] = mixed[:, 0:CH].astype(BF16)
        total = mixed[:, CH + 4 : CH + 5]
        high = total.astype(BF16).astype(F32)
        notes = jnp.where(wide_lane == 4, high, 0.0)
        notes = jnp.where(wide_lane == 5, largest, notes)
        notes = jnp.where(wide_lane == 6, total - high, notes)
        sent[d, :, CH:EXT] = notes.astype(BF16)

    def part_copy(d):
        return remote(
            sent.at[d], parts.at[d], part_send.at[d], part_recv.at[d], tile_at(x + d, y, z), frame
        )

    def each_part(n, carry):
        d = 3 - n
        attend(d)

        @pl.when(d > 0)
        def _():
            part_copy(d).start()

        return carry

    lax.fori_loop(0, 4, each_part, 0)
    for d in range(3, 0, -1):
        part_copy(d).wait_recv()

    def part(d, lanes):
        return (sent[0, :, lanes] if d == 0 else parts[d, :, lanes]).astype(F32)

    tails = [part(d, pl.ds(CH, LANES)) for d in range(4)]
    maxima = [tail[:, 5:6] for tail in tails]
    most = functools.reduce(jnp.maximum, maxima)
    factors = [jnp.exp2(m - most) for m in maxima]
    denominator = sum((t[:, 4:5] + t[:, 6:7]) * f for t, f in zip(tails, factors))
    numerator = sum(part(d, pl.ds(0, CH)) * factors[d] for d in range(4))
    averaged = (numerator / denominator).astype(BF16)
    mixed = jnp.dot(averaged, triple_weight[:, 2 * CH : 3 * CH], preferred_element_type=F32)
    mixed = (mixed + line_of(triple_bias, 2)).astype(BF16)
    attended = jnp.dot(mixed, output_weight[...], preferred_element_type=F32)
    total = own[...].astype(F32) + attended + line_of(output_bias)
    rows = []
    for r in range(ROWS):
        rows.append(
            jnp.where(column < width_of(first + r), total[r * COLS : (r + 1) * COLS], 0.0)
        )
    rim[...] = jnp.concatenate(rows, axis=0).astype(BF16)
    up = remote(
        rim.at[pl.ds(0, WIDE)], rim_bot, rim_send.at[0], rim_recv.at[0], tile - 1, frame
    )
    down = remote(
        rim.at[pl.ds(LAST, WIDE)], rim_top, rim_send.at[1], rim_recv.at[1], tile + 1, frame
    )

    @pl.when(above)
    def _():
        up.start()

    @pl.when(below)
    def _():
        down.start()

    def product(k, carry):
        taps[k, :, 0:OUT] = lax.dot_general(
            rim[...], up_weight[k], NT, preferred_element_type=F32
        )
        return carry

    lax.fori_loop(0, 9, product, 0)

    @pl.when(below)
    def _():
        up.wait_recv()
        down.wait_send()

    @pl.when(above)
    def _():
        down.wait_recv()
        up.wait_send()

    for e in range(3):
        ends[e, :, 0:OUT] = lax.dot_general(
            rim_top[...], up_weight[e], NT, preferred_element_type=F32
        )
        ends[3 + e, :, 0:OUT] = lax.dot_general(
            rim_bot[...], up_weight[6 + e], NT, preferred_element_type=F32
        )
    up_column = lax.broadcasted_iota(jnp.int32, (COLS, 2 * LANES), 0)
    for r in range(ROWS):
        label = label_of(first + r)
        lines = pl.ds(r * COLS, COLS)
        for p in range(2):
            joined = []
            other = r - 1 if p == 0 else r + 1
            alike = label_of(first + other) == label
            outer = 0 if p == 0 else 2
            for e in range(3):
                if other < 0:
                    far = ends[e, WIDE - COLS :, :]
                elif other == ROWS:
                    far = ends[3 + e, :COLS, :]
                else:
                    far = taps[outer * 3 + e, pl.ds(other * COLS, COLS), :]
                near = taps[3 + e, lines, :] + taps[(2 - outer) * 3 + e, lines, :]
                joined.append(near + jnp.where(alike, far, 0.0))
            before = jnp.where(up_column == 0, 0.0, pltpu.roll(joined[0], 1, 0))
            after = jnp.where(up_column == COLS - 1, 0.0, pltpu.roll(joined[2], COLS - 1, 0))
            valid = up_column < width_of(first + r)
            left = before + joined[1] + joined[2] + wide_bias[...]
            right = joined[0] + joined[1] + after + wide_bias[...]
            left = jnp.where(valid, left, 0.0)
            right = jnp.where(valid, right, 0.0)
            for half, lanes in ((low, slice(0, LANES)), (high, slice(LANES, 2 * LANES))):
                half[pl.ds(0, COLS, stride=2), :] = left[:, lanes]
                half[pl.ds(1, COLS, stride=2), :] = right[:, lanes]
            out[2 * r + p, :, 0:LANES] = low[...].astype(BF16)
            out[2 * r + p, :, LANES:OUT] = high[:, 0 : OUT - LANES].astype(BF16)

    @pl.when(next_frame)
    def _():
        to_next.wait_send()
        tab_next.wait_send()

    @pl.when(frame + 2 < FRAMES)
    def _():
        tab_skip.wait_send()

    @pl.when(skip_frame)
    def _():
        to_skip.wait_send()

    @pl.when(relay)
    def _():
        to_relay.wait_send()

    end_halo(2)

    @pl.when(has[1])
    def _():
        end_halo(1)

    @pl.when(has[0])
    def _():
        end_halo(0)
    all_sums(0).wait_send()
    all_sums(1).wait_send()
    for copy in kv_copies + q_copies:
        copy.wait_send()
    for d in range(3, 0, -1):
        part_copy(d).wait_send()


def shards(
    latents,
    row_video,
    video_cols,
    first_gain,
    first_shift,
    conv_weight,
    conv_bias,
    second_gain,
    second_shift,
    triple_weight,
    triple_bias,
    output_weight,
    output_bias,
    upsample_weight,
    upsample_bias,
):
    smem = pl.BlockSpec(memory_space=pltpu.SMEM)
    vmem = pl.BlockSpec(memory_space=pltpu.VMEM)
    anywhere = pl.BlockSpec(memory_space=pl.ANY)
    dma = pltpu.SemaphoreType.DMA
    block = (CELLS, CH)
    edge = (WIDE, CH)
    decoded = pl.pallas_call(
        whole_kernel,
        out_shape=jax.ShapeDtypeStruct((2 * ROWS, 2 * COLS, OUT), BF16),
        in_specs=[smem, smem, anywhere, vmem, vmem, anywhere] + [vmem] * 9,
        out_specs=vmem,
        scratch_shapes=[
            pltpu.VMEM(block, BF16),
            pltpu.VMEM((2,) + block, BF16),
            pltpu.VMEM((3,) + edge, BF16),
            pltpu.VMEM((3,) + edge, BF16),
            pltpu.VMEM((2, TILES, 8, LANES), F32),
            pltpu.VMEM((TILES * 8, LANES), F32),
            pltpu.VMEM((TILES * 8, LANES), F32),
            pltpu.VMEM((8, CH), F32),
            pltpu.VMEM((3, 16, CH), F32),
            pltpu.VMEM((3, 6 * WIDE, 3 * CH), BF16),
            pltpu.VMEM((9, 3 * CH, CH), BF16),
            pltpu.VMEM((3, PADDED, CH), F32),
            pltpu.VMEM(block, BF16),
            pltpu.VMEM((8,) + block, BF16),
            pltpu.VMEM((3,) + block, BF16),
            pltpu.VMEM((16, CH), F32),
            pltpu.VMEM((KEYS, EXT), BF16),
            pltpu.VMEM((4, CELLS, EXT), BF16),
            pltpu.VMEM((CELLS, KEYS), F32),
            pltpu.VMEM((4, CELLS, EXT), BF16),
            pltpu.VMEM((4, CELLS, EXT), BF16),
            pltpu.VMEM(block, BF16),
            pltpu.VMEM(edge, BF16),
            pltpu.VMEM(edge, BF16),
            pltpu.VMEM((9, CELLS, 2 * LANES), F32),
            pltpu.VMEM((6, WIDE, 2 * LANES), F32),
            pltpu.VMEM((2 * COLS, LANES), F32),
            pltpu.VMEM((2 * COLS, LANES), F32),
            pltpu.VMEM((1, 2 * LANES), F32),
            dma((2,)),
            dma((2,)),
            dma((3,)),
            dma((2,)),
            dma((3, 2)),
            dma((3, 2)),
            dma((2,)),
            dma((2,)),
            dma((2,)),
            dma((9,)),
            dma((9,)),
            dma((3,)),
            dma((3,)),
            dma((4,)),
            dma((4,)),
            dma((2,)),
            dma((2,)),
        ],
        compiler_params=pltpu.CompilerParams(
            collective_id=0, has_side_effects=True, vmem_limit_bytes=56 * 2**20
        ),
        name="decoder_window",
    )(
        row_video, video_cols, latents.reshape(CELLS, CH), first_gain, first_shift,
        conv_weight.reshape(9, 3 * CH, CH), conv_bias, second_gain, second_shift, triple_weight,
        triple_bias, output_weight, output_bias,
        jnp.transpose(upsample_weight, (0, 1, 3, 2)).reshape(9, OUT, CH), upsample_bias,
    )
    return decoded.reshape(2 * ROWS, 1, 2 * COLS, OUT)


def solution(mesh):
    in_specs = (P("tile", "frame", None, None),) + (P(),) * 14
    out_specs = P("tile", "frame", None, None)
    return jax.shard_map(shards, mesh=mesh, in_specs=in_specs, out_specs=out_specs, check_vma=False)
```

time: 144 us -> 106 us (0.74)
  Pallas kernels: 128 us -> 104 us
  local copies, waits for them, and re-layouts: 14.1 us -> 2.18 us
  other arithmetic: 1.68 us -> 0 us
    pallas_call x3 -> x1, Pallas kernels: 128 us -> 104 us  [shards(): pl.pallas_call(whole_kernel, out_shape=jax.ShapeDtypeStruct((2 * ROWS, 2...]
    unnamed x11 -> x0, local copies, waits for them, and re-layouts: 5.35 us -> none
    reshape x7 -> x0, local copies, waits for them, and re-layouts: 4.8 us -> none  [line(): return vector.reshape(1, -1)]
    reduce_sum x2 -> x0, other arithmetic: 1.52 us -> none  [the longest x1 0.77 us: shards(): jnp.sum(jnp.where(matches, canvas_widths[:, None], 0), axis=0) * per_group]
    pad x3 -> x0, local copies, waits for them, and re-layouts: 1.49 us -> none  [the longest x1 0.73 us: shards(): labels = jnp.pad(row_video, 1, constant_values=-1)]
where the time goes in v3:
time: 106 us
  Pallas kernels  104 us (98%)
  local copies, waits for them, and re-layouts  2.18 us (2%)
    pallas_call x1, Pallas kernels, shards(): pl.pallas_call(whole_kernel, out_shape=jax.ShapeDtypeStruct((2 * ROWS, 2...  104 us
    reshape x1, local copies, waits for them, and re-layouts, shards(): return decoded.reshape(2 * ROWS, 1, 2 * COLS, OUT)  2.18 us

profile of v3, /device:TPU:66, one launch (start us, length us, event | category | flops | bytes accessed | tf_op | source)
XLA Modules:
  0.0 105.7 jit_solution(15717305007646351698)
XLA Ops:
  0.0 103.5 %decoder_window.1 = bf16[8,208,192]{2,1,0:T(8,128)(2,1)} custom-call(s32[128]{0:T(128)} %videos.1, s32[4]{0:T(128)} %cols.1, bf16[416,384]{1,0:T(8,128)(2,1)} %bitcast.9, f32[384]{0:T(512)} %first_gain.1, f32[384]{0:T(512)} %first_shift.1, bf16[9,1152,384]{2,1,0:T(8,128)(2,1)} %bitcast.6, f32[384]{0:T(512)} %conv_bias.1, f32[384]{0:T(512)} %second_gain.1, ...), custom_call_target="tpu_custom_call" | custom-call | tf_op jit(solution)/shard_map/decoder_window/pallas_call | solution.py:698
  103.5 2.2 %copy.16 = bf16[8,1,208,192]{2,3,1,0:T(8,128)(2,1)} copy(bf16[8,1,208,192]{3,2,0,1:T(8,128)(2,1)} %bitcast.7) | data formatting | bytes 1277952 | tf_op jit(solution)/shard_map/reshape | solution.py:761

commit v4 on v3

--- a/solution.py
+++ b/solution.py
@@ -134,10 +134,11 @@
     videos, cols, lat_hbm, first_gain, first_shift, conv_hbm, conv_bias, second_gain, second_shift,
     triple_weight, triple_bias, output_weight, output_bias, up_weight, up_bias, out,
     lat, main, top, bot, gat, onehot, row_cells, st, tabs, hid, weight, acc,
-    own, kv, qb, tab, keys, queries, scores, sent, parts, rim, rim_top, rim_bot,
+    own, kv, qb, tab, keys, queries, scores, sent, parts, sent_notes, part_notes, rim, rim_top, rim_bot,
     taps, ends, low, high, wide_bias,
     stat_send, stat_recv, main_send, main_recv, halo_send, halo_recv, tab_send, tab_recv,
-    load_sem, kv_send, kv_recv, q_send, q_recv, part_send, part_recv, rim_send, rim_recv,
+    load_sem, kv_send, kv_recv, q_send, q_recv, part_send, part_recv, note_send, note_recv,
+    rim_send, rim_recv,
 ):
     tile, frame, x, y, z = place()
     first = tile * ROWS
@@ -168,6 +169,16 @@
         @pl.when(there)
         def _():
             greet(barrier, tile, frame + step)
+
+        awaited = awaited + there.astype(jnp.int32)
+
+    partner = frame + 1 - 2 * lax.rem(frame, 2)
+    for step in (-1, 1):
+        there = (tile + step >= 0) & (tile + step < TILES)
+
+        @pl.when(there)
+        def _():
+            greet(barrier, tile + step, partner)
 
         awaited = awaited + there.astype(jnp.int32)
 
@@ -225,9 +236,28 @@
     above = tile >= 1
     below = tile + 1 < TILES
 
-    to_next = remote(lat, main.at[1], main_send.at[1], main_recv.at[1], tile, frame + 1)
-    to_skip = remote(lat, main.at[0], main_send.at[0], main_recv.at[0], tile, frame + 2)
-    to_relay = remote(main.at[1], main.at[0], main_send.at[2], main_recv.at[0], tile, frame + 1)
+    pieces = (pl.ds(0, WIDE), pl.ds(LAST, WIDE), pl.ds(WIDE, LAST - WIDE))
+
+    def frame_copies(kind, src, a, to_frame):
+        return [
+            remote(
+                src.at[p], main.at[a].at[p], main_send.at[kind, i], main_recv.at[a, i], tile,
+                to_frame,
+            )
+            for i, p in enumerate(pieces)
+        ]
+
+    to_next = frame_copies(1, lat, 1, frame + 1)
+    to_skip = frame_copies(0, lat, 0, frame + 2)
+    to_relay = frame_copies(2, main.at[1], 0, frame + 1)
+    diagonal_up = remote(
+        main.at[1].at[pieces[0]], bot.at[0], halo_send.at[3, 0], halo_recv.at[0, 0], tile - 1,
+        frame + 1,
+    )
+    diagonal_down = remote(
+        main.at[1].at[pieces[1]], top.at[0], halo_send.at[3, 1], halo_recv.at[0, 1], tile + 1,
+        frame + 1,
+    )
 
     def halo(a):
         src = lat if a == 2 else main.at[a]
@@ -276,7 +306,8 @@
 
     @pl.when(next_frame)
     def _():
-        to_next.start()
+        for copy in to_next:
+            copy.start()
 
     start_halo(2)
 
@@ -284,7 +315,8 @@
 
     @pl.when(skip_frame)
     def _():
-        to_skip.start()
+        for copy in to_skip:
+            copy.start()
 
     mean, scale = combine_sums(gat[0], onehot[...], row_cells[...])
     tabs[2, 0:8, :] = mean
@@ -307,7 +339,8 @@
         width = width_of(first - 1 + row)
         row_mean, row_scale = pick(tabs[a], label)
         normed = (cells - row_mean) * row_scale * line_of(first_gain) + line_of(first_shift)
-        hidden = normed / (1.0 + jnp.exp(-normed))
+        half_normed = 0.5 * normed
+        hidden = half_normed + half_normed * jnp.tanh(half_normed)
         hidden = jnp.where(column < width, hidden, 0.0)
         hidden = jnp.concatenate([hidden, jnp.zeros((WIDE - COLS, CH), F32)], axis=0)
         lines = pl.ds(row * WIDE, WIDE)
@@ -336,39 +369,63 @@
 
         lax.fori_loop(0, 3, tap, 0)
 
+    @pl.when(has[1])
+    def _():
+        to_next[0].wait_recv()
+        to_next[1].wait_recv()
+        start_halo(1)
+
+    @pl.when(relay)
+    def _():
+        to_relay[0].start()
+        to_relay[1].start()
+
+    @pl.when(relay & above)
+    def _():
+        diagonal_up.start()
+
+    @pl.when(relay & below)
+    def _():
+        diagonal_down.start()
+
     activate_main(2)
+
+    @pl.when(relay)
+    def _():
+        to_next[2].wait_recv()
+        to_relay[2].start()
+
     wait_halo(2)
     activate_halo(2)
     load.wait()
     convolve(2)
 
+    @pl.when(has[1] & jnp.logical_not(relay))
+    def _():
+        to_next[2].wait_recv()
+
+    @pl.when(relay)
+    def _():
+        to_skip[0].wait_recv()
+        to_skip[1].wait_recv()
+        start_halo(0)
+
     @pl.when(has[1])
     def _():
-        to_next.wait_recv()
-
-    @pl.when(relay)
-    def _():
-        to_relay.start()
-
-    @pl.when(has[1])
-    def _():
-        start_halo(1)
         tab_next.wait_recv()
         activate_main(1)
-
-    @pl.when(has[0])
-    def _():
-        to_skip.wait_recv()
-        start_halo(0)
-
-    @pl.when(has[1])
-    def _():
         wait_halo(1)
         activate_halo(1)
         convolve(1)
 
+    @pl.when(has[0] & jnp.logical_not(relay))
+    def _():
+        to_skip[0].wait_recv()
+        to_skip[1].wait_recv()
+
     @pl.when(has[0])
     def _():
+        to_skip[2].wait_recv()
         tab_skip.wait_recv()
         activate_main(0)
         wait_halo(0)
@@ -485,14 +542,6 @@
     for copy in relays[0][1]:
         copy.start()
     put_keys(4, kv[4], across)
-    for d in range(1, 4):
-        q_copies[d - 1].wait_recv()
-
-    def each_query(d, carry):
-        put_query(d, qb[d - 1], tile_at(x + 4 - d, y, z))
-        return carry
-
-    lax.fori_loop(1, 4, each_query, 0)
 
     def put_pair(low_slot):
         def each_key(n, carry):
@@ -508,6 +557,14 @@
     for copy in relays[1][1]:
         copy.start()
     put_pair(5)
+    for d in range(1, 4):
+        q_copies[d - 1].wait_recv()
+
+    def each_query(d, carry):
+        put_query(d, qb[d - 1], tile_at(x + 4 - d, y, z))
+        return carry
+
+    lax.fori_loop(1, 4, each_query, 0)
     for zz in range(2):
         for copy in relays[zz][1]:
             copy.wait_recv()
@@ -517,45 +574,56 @@
         slot = lax.rem(4 - d, 4)
         scores[...] = lax.dot_general(queries[slot], keys[...], NT, preferred_element_type=F32)
         held = scores[...]
-        largest = jnp.max(held, axis=1, keepdims=True).astype(BF16).astype(F32)
+        largest = jnp.max(held, axis=1, keepdims=True)
         weights = jnp.exp2(held - largest).astype(BF16)
         mixed = jnp.dot(weights, keys[...], preferred_element_type=F32)
-        sent[d, :, 0:CH] = mixed[:, 0:CH].astype(BF16)
-        total = mixed[:, CH + 4 : CH + 5]
-        high = total.astype(BF16).astype(F32)
-        notes = jnp.where(wide_lane == 4, high, 0.0)
-        notes = jnp.where(wide_lane == 5, largest, notes)
-        notes = jnp.where(wide_lane == 6, total - high, notes)
-        sent[d, :, CH:EXT] = notes.astype(BF16)
+        sent[d] = mixed[:, 0:CH].astype(BF16)
+        notes = jnp.where(wide_lane == 0, mixed[:, CH + 4 : CH + 5], 0.0)
+        notes = jnp.where(wide_lane == 1, largest, notes)
+        notes = jnp.concatenate([notes, jnp.zeros((4 * LANES - CELLS, LANES), F32)], axis=0)
+        sent_notes[d] = jnp.transpose(notes)[0:8]
 
     def part_copy(d):
         return remote(
             sent.at[d], parts.at[d], part_send.at[d], part_recv.at[d], tile_at(x + d, y, z), frame
         )
 
+    def note_copy(d):
+        return remote(
+            sent_notes.at[d], part_notes.at[d], note_send.at[d], note_recv.at[d],
+            tile_at(x + d, y, z), frame,
+        )
+
     def each_part(n, carry):
         d = 3 - n
         attend(d)
 
         @pl.when(d > 0)
         def _():
+            note_copy(d).start()
             part_copy(d).start()
 
         return carry
 
     lax.fori_loop(0, 4, each_part, 0)
     for d in range(3, 0, -1):
+        note_copy(d).wait_recv()
         part_copy(d).wait_recv()
 
-    def part(d, lanes):
-        return (sent[0, :, lanes] if d == 0 else parts[d, :, lanes]).astype(F32)
-
-    tails = [part(d, pl.ds(CH, LANES)) for d in range(4)]
-    maxima = [tail[:, 5:6] for tail in tails]
+    def part(d):
+        return (sent[0] if d == 0 else parts[d]).astype(F32)
+
+    def note(d):
+        held = sent_notes[0] if d == 0 else part_notes[d]
+        held = jnp.concatenate([held, jnp.zeros((LANES - 8, 4 * LANES), F32)], axis=0)
+        return jnp.transpose(held)[:CELLS]
+
+    tails = [note(d) for d in range(4)]
+    maxima = [tail[:, 1:2] for tail in tails]
     most = functools.reduce(jnp.maximum, maxima)
     factors = [jnp.exp2(m - most) for m in maxima]
-    denominator = sum((t[:, 4:5] + t[:, 6:7]) * f for t, f in zip(tails, factors))
-    numerator = sum(part(d, pl.ds(0, CH)) * factors[d] for d in range(4))
+    denominator = sum(t[:, 0:1] * f for t, f in zip(tails, factors))
+    numerator = sum(part(d) * factors[d] for d in range(4))
     averaged = (numerator / denominator).astype(BF16)
     mixed = jnp.dot(averaged, triple_weight[:, 2 * CH : 3 * CH], preferred_element_type=F32)
     mixed = (mixed + line_of(triple_bias, 2)).astype(BF16)
@@ -640,7 +708,8 @@
 
     @pl.when(next_frame)
     def _():
-        to_next.wait_send()
+        for copy in to_next:
+            copy.wait_send()
         tab_next.wait_send()
 
     @pl.when(frame + 2 < FRAMES)
@@ -649,11 +718,22 @@
 
     @pl.when(skip_frame)
     def _():
-        to_skip.wait_send()
+        for copy in to_skip:
+            copy.wait_send()
 
     @pl.when(relay)
     def _():
-        to_relay.wait_send()
+        for copy in to_relay:
+            copy.wait_send()
+        end_halo(0)
+
+    @pl.when(relay & above)
+    def _():
+        diagonal_up.wait_send()
+
+    @pl.when(relay & below)
+    def _():
+        diagonal_down.wait_send()
 
     end_halo(2)
 
@@ -661,15 +741,13 @@
     def _():
         end_halo(1)
 
-    @pl.when(has[0])
-    def _():
-        end_halo(0)
     all_sums(0).wait_send()
     all_sums(1).wait_send()
     for copy in kv_copies + q_copies:
         copy.wait_send()
     for d in range(3, 0, -1):
         part_copy(d).wait_send()
+        note_copy(d).wait_send()
 
 
 def shards(
@@ -720,8 +798,10 @@
             pltpu.VMEM((KEYS, EXT), BF16),
             pltpu.VMEM((4, CELLS, EXT), BF16),
             pltpu.VMEM((CELLS, KEYS), F32),
-            pltpu.VMEM((4, CELLS, EXT), BF16),
-            pltpu.VMEM((4, CELLS, EXT), BF16),
+            pltpu.VMEM((4,) + block, BF16),
+            pltpu.VMEM((4,) + block, BF16),
+            pltpu.VMEM((4, 8, 4 * LANES), F32),
+            pltpu.VMEM((4, 8, 4 * LANES), F32),
             pltpu.VMEM(block, BF16),
             pltpu.VMEM(edge, BF16),
             pltpu.VMEM(edge, BF16),
@@ -732,9 +812,9 @@
             pltpu.VMEM((1, 2 * LANES), F32),
             dma((2,)),
             dma((2,)),
-            dma((3,)),
-            dma((2,)),
-            dma((3, 2)),
+            dma((3, 3)),
+            dma((2, 3)),
+            dma((4, 2)),
             dma((3, 2)),
             dma((2,)),
             dma((2,)),
@@ -743,6 +823,8 @@
             dma((9,)),
             dma((3,)),
             dma((3,)),
+            dma((4,)),
+            dma((4,)),
             dma((4,)),
             dma((4,)),
             dma((2,)),

time: 106 us -> 97.2 us (0.917)
  Pallas kernels: 104 us -> 94.9 us
    pallas_call x1, Pallas kernels: 104 us -> 94.9 us  [shards(): pl.pallas_call(whole_kernel, out_shape=jax.ShapeDtypeStruct((2 * ROWS, 2...]
where the time goes in v4:
time: 97.2 us; the launch traced here: 97.1 us
  Pallas kernels  94.9 us (98%)
  local copies, waits for them, and re-layouts  2.18 us (2%)
    pallas_call x1, Pallas kernels, shards(): pl.pallas_call(whole_kernel, out_shape=jax.ShapeDtypeStruct((2 * ROWS, 2...  94.9 us
    reshape x1, local copies, waits for them, and re-layouts, shards(): return decoded.reshape(2 * ROWS, 1, 2 * COLS, OUT)  2.18 us

profile of v4, /device:TPU:66, one launch (start us, length us, event | category | flops | bytes accessed | tf_op | source)
XLA Modules:
  0.0 97.1 jit_solution(17289074776959567498)
XLA Ops:
  0.0 94.9 %decoder_window.1 = bf16[8,208,192]{2,1,0:T(8,128)(2,1)} custom-call(s32[128]{0:T(128)} %videos.1, s32[4]{0:T(128)} %cols.1, bf16[416,384]{1,0:T(8,128)(2,1)} %bitcast.9, f32[384]{0:T(512)} %first_gain.1, f32[384]{0:T(512)} %first_shift.1, bf16[9,1152,384]{2,1,0:T(8,128)(2,1)} %bitcast.6, f32[384]{0:T(512)} %conv_bias.1, f32[384]{0:T(512)} %second_gain.1, ...), custom_call_target="tpu_custom_call" | custom-call | tf_op jit(solution)/shard_map/decoder_window/pallas_call | solution.py:776
  94.9 2.2 %copy.16 = bf16[8,1,208,192]{2,3,1,0:T(8,128)(2,1)} copy(bf16[8,1,208,192]{3,2,0,1:T(8,128)(2,1)} %bitcast.7) | data formatting | bytes 1277952 | tf_op jit(solution)/shard_map/reshape | solution.py:843

commit v5 on v4

--- a/solution.py
+++ b/solution.py
@@ -132,8 +132,8 @@
 
 def whole_kernel(
     videos, cols, lat_hbm, first_gain, first_shift, conv_hbm, conv_bias, second_gain, second_shift,
-    triple_weight, triple_bias, output_weight, output_bias, up_weight, up_bias, out,
-    lat, main, top, bot, gat, onehot, row_cells, st, tabs, hid, weight, acc,
+    triple_hbm, triple_bias, output_hbm, output_bias, up_hbm, up_bias, out,
+    triple_weight, output_weight, up_weight, lat, main, top, bot, gat, onehot, row_cells, st, tabs, hid, weight, acc,
     own, kv, qb, tab, keys, queries, scores, sent, parts, sent_notes, part_notes, rim, rim_top, rim_bot,
     taps, ends, low, high, wide_bias,
     stat_send, stat_recv, main_send, main_recv, halo_send, halo_recv, tab_send, tab_recv,
@@ -146,6 +146,13 @@
     load_lat.start()
     load = pltpu.make_async_copy(conv_hbm, weight, load_sem.at[1])
     load.start()
+    load_rest = [
+        pltpu.make_async_copy(triple_hbm, triple_weight, load_sem.at[2]),
+        pltpu.make_async_copy(output_hbm, output_weight, load_sem.at[3]),
+        pltpu.make_async_copy(up_hbm, up_weight, load_sem.at[4]),
+    ]
+    for copy in load_rest:
+        copy.start()
 
     def label_of(row):
         inside = (row >= 0) & (row < TILES * ROWS)
@@ -444,43 +451,51 @@
         rows.append(jnp.where(column < width_of(first + r), total, 0.0))
     own[...] = jnp.concatenate(rows, axis=0).astype(BF16)
 
-    source = own[...].astype(F32)
-    gat[1, tile] = local_sums(source, width_of, first, st)
-    send_sums(1)
-
     half = CELLS // 2
-    upper_half, lower_half = pl.ds(0, half), pl.ds(half, half)
+    halves = (pl.ds(0, half), pl.ds(half, half))
     ahead, behind, across = tile_at(x, y + 1, z), tile_at(x, y + 3, z), tile_at(x, y, z + 1)
 
-    def pass_on(k, src, slot, peer, lines=None):
-        dst = kv.at[slot]
-        if lines is not None:
-            src, dst = src.at[lines], dst.at[lines]
-        return remote(src, dst, kv_send.at[k], kv_recv.at[k], peer, frame)
-
-    kv_across = pass_on(0, own, 4, across)
-    kv_copies = [kv_across]
-    relays = []
+    def pass_on(src, slot, h, peer):
+        return remote(
+            src.at[halves[h]], kv.at[slot].at[halves[h]], kv_send.at[slot, h],
+            kv_recv.at[slot, h], peer, frame,
+        )
+
+    kv_across = [pass_on(own, 4, h, across) for h in range(2)]
+    kv_copies = list(kv_across)
+    to_ahead, to_behind, relays = [], [], []
     for zz in range(2):
         base = own if zz == 0 else kv.at[4]
-        near = (pass_on(1 + 4 * zz, base, zz * 4 + 1, ahead),
-                pass_on(2 + 4 * zz, base, zz * 4 + 3, behind))
-        far = (pass_on(3 + 4 * zz, kv.at[zz * 4 + 1], zz * 4 + 2, ahead, upper_half),
-               pass_on(4 + 4 * zz, kv.at[zz * 4 + 3], zz * 4 + 2, behind, lower_half))
-        relays.append((near, far))
-        kv_copies += list(near) + list(far)
+        to_ahead.append([pass_on(base, zz * 4 + 1, h, ahead) for h in range(2)])
+        to_behind.append([pass_on(base, zz * 4 + 3, h, behind) for h in range(2)])
+        relays.append([pass_on(kv.at[zz * 4 + 1], zz * 4 + 2, 0, ahead),
+                       pass_on(kv.at[zz * 4 + 3], zz * 4 + 2, 1, behind)])
+        kv_copies += to_ahead[zz] + to_behind[zz] + relays[zz]
     q_copies = []
     for d in range(1, 4):
         peer = tile_at(x + d, y, z)
         q_copies.append(remote(own, qb.at[d - 1], q_send.at[d - 1], q_recv.at[d - 1], peer, frame))
-    kv_across.start()
-    for copy in relays[0][0]:
-        copy.start()
+    kv_across[0].start()
+    to_ahead[0][0].start()
+    to_behind[0][1].start()
+    kv_across[1].start()
+    to_ahead[0][1].start()
+    to_behind[0][0].start()
     for copy in q_copies:
         copy.start()
-    kv_across.wait_recv()
-    for copy in relays[1][0]:
-        copy.start()
+    source = own[...].astype(F32)
+    gat[1, tile] = local_sums(source, width_of, first, st)
+    send_sums(1)
+    kv_across[0].wait_recv()
+    to_ahead[1][0].start()
+    kv_across[1].wait_recv()
+    to_behind[1][1].start()
+    to_ahead[0][0].wait_recv()
+    relays[0][0].start()
+    to_behind[0][1].wait_recv()
+    relays[0][1].start()
+    to_ahead[1][1].start()
+    to_behind[1][0].start()
     all_sums(1).wait_recv()
     mean, scale = combine_sums(gat[1], onehot[...], row_cells[...])
     tab[0:8, :] = mean
@@ -535,13 +550,13 @@
     def key_tile(slot):
         return tile_at(x, y + 4 - lax.rem(slot, 4), z + lax.div(slot, 4))
 
+    for copy in load_rest:
+        copy.wait()
     put_query(0, own[...], tile)
     put_keys(0, own[...], tile)
-    for copy in relays[0][0]:
-        copy.wait_recv()
-    for copy in relays[0][1]:
-        copy.start()
     put_keys(4, kv[4], across)
+    to_ahead[0][1].wait_recv()
+    to_behind[0][0].wait_recv()
 
     def put_pair(low_slot):
         def each_key(n, carry):
@@ -552,11 +567,10 @@
         lax.fori_loop(0, 2, each_key, 0)
 
     put_pair(1)
-    for copy in relays[1][0]:
-        copy.wait_recv()
-    for copy in relays[1][1]:
-        copy.start()
-    put_pair(5)
+    to_ahead[1][0].wait_recv()
+    relays[1][0].start()
+    to_behind[1][1].wait_recv()
+    relays[1][1].start()
     for d in range(1, 4):
         q_copies[d - 1].wait_recv()
 
@@ -565,8 +579,11 @@
         return carry
 
     lax.fori_loop(1, 4, each_query, 0)
+    to_ahead[1][1].wait_recv()
+    to_behind[1][0].wait_recv()
+    put_pair(5)
     for zz in range(2):
-        for copy in relays[zz][1]:
+        for copy in relays[zz]:
             copy.wait_recv()
         put_keys(zz * 4 + 2, kv[zz * 4 + 2], key_tile(jnp.int32(zz * 4 + 2)))
 
@@ -776,9 +793,13 @@
     decoded = pl.pallas_call(
         whole_kernel,
         out_shape=jax.ShapeDtypeStruct((2 * ROWS, 2 * COLS, OUT), BF16),
-        in_specs=[smem, smem, anywhere, vmem, vmem, anywhere] + [vmem] * 9,
+        in_specs=[smem, smem, anywhere, vmem, vmem, anywhere, vmem, vmem, vmem]
+        + [anywhere, vmem] * 3,
         out_specs=vmem,
         scratch_shapes=[
+            pltpu.VMEM((CH, 3 * CH), BF16),
+            pltpu.VMEM((CH, CH), BF16),
+            pltpu.VMEM((9, OUT, CH), BF16),
             pltpu.VMEM(block, BF16),
             pltpu.VMEM((2,) + block, BF16),
             pltpu.VMEM((3,) + edge, BF16),
@@ -818,9 +839,9 @@
             dma((3, 2)),
             dma((2,)),
             dma((2,)),
-            dma((2,)),
-            dma((9,)),
-            dma((9,)),
+            dma((5,)),
+            dma((8, 2)),
+            dma((8, 2)),
             dma((3,)),
             dma((3,)),
             dma((4,)),

time: 97.2 us -> 98.2 us (1.010)
  Pallas kernels: 94.9 us -> 95.9 us
where the time goes in v5:
time: 98.2 us; the launch traced here: 98.1 us
  Pallas kernels  95.9 us (98%)
  local copies, waits for them, and re-layouts  2.18 us (2%)
    pallas_call x1, Pallas kernels, shards(): pl.pallas_call(whole_kernel, out_shape=jax.ShapeDtypeStruct((2 * ROWS, 2...  95.9 us
    reshape x1, local copies, waits for them, and re-layouts, shards(): return decoded.reshape(2 * ROWS, 1, 2 * COLS, OUT)  2.18 us

profile of v5, /device:TPU:66, one launch (start us, length us, event | category | flops | bytes accessed | tf_op | source)
XLA Modules:
  0.0 98.1 jit_solution(13983464307731250119)
XLA Ops:
  0.0 95.9 %decoder_window.1 = bf16[8,208,192]{2,1,0:T(8,128)(2,1)} custom-call(s32[128]{0:T(128)} %videos.1, s32[4]{0:T(128)} %cols.1, bf16[416,384]{1,0:T(8,128)(2,1)} %bitcast.9, f32[384]{0:T(512)} %first_gain.1, f32[384]{0:T(512)} %first_shift.1, bf16[9,1152,384]{2,1,0:T(8,128)(2,1)} %bitcast.6, f32[384]{0:T(512)} %conv_bias.1, f32[384]{0:T(512)} %second_gain.1, ...), custom_call_target="tpu_custom_call" | custom-call | tf_op jit(solution)/shard_map/decoder_window/pallas_call | solution.py:793
  95.9 2.2 %copy.16 = bf16[8,1,208,192]{2,3,1,0:T(8,128)(2,1)} copy(bf16[8,1,208,192]{3,2,0,1:T(8,128)(2,1)} %bitcast.7) | data formatting | bytes 1277952 | tf_op jit(solution)/shard_map/reshape | solution.py:864

commit v6 on v5

--- a/solution.py
+++ b/solution.py
@@ -475,6 +475,9 @@
     for d in range(1, 4):
         peer = tile_at(x + d, y, z)
         q_copies.append(remote(own, qb.at[d - 1], q_send.at[d - 1], q_recv.at[d - 1], peer, frame))
+    source = own[...].astype(F32)
+    gat[1, tile] = local_sums(source, width_of, first, st)
+    send_sums(1)
     kv_across[0].start()
     to_ahead[0][0].start()
     to_behind[0][1].start()
@@ -483,23 +486,20 @@
     to_behind[0][0].start()
     for copy in q_copies:
         copy.start()
-    source = own[...].astype(F32)
-    gat[1, tile] = local_sums(source, width_of, first, st)
-    send_sums(1)
     kv_across[0].wait_recv()
     to_ahead[1][0].start()
     kv_across[1].wait_recv()
     to_behind[1][1].start()
+    all_sums(1).wait_recv()
+    mean, scale = combine_sums(gat[1], onehot[...], row_cells[...])
+    tab[0:8, :] = mean
+    tab[8:16, :] = scale
     to_ahead[0][0].wait_recv()
     relays[0][0].start()
     to_behind[0][1].wait_recv()
     relays[0][1].start()
     to_ahead[1][1].start()
     to_behind[1][0].start()
-    all_sums(1).wait_recv()
-    mean, scale = combine_sums(gat[1], onehot[...], row_cells[...])
-    tab[0:8, :] = mean
-    tab[8:16, :] = scale
     column = lax.broadcasted_iota(jnp.int32, (COLS, CH), 0)
     cell_column = lax.broadcasted_iota(jnp.int32, (COLS, LANES), 0)
     lane = lax.broadcasted_iota(jnp.int32, (COLS, LANES), 1)
@@ -612,7 +612,7 @@
         )
 
     def each_part(n, carry):
-        d = 3 - n
+        d = jnp.where(n < 2, 2 + n, 3 - n)
         attend(d)
 
         @pl.when(d > 0)

time: 98.2 us -> 94.3 us (0.960)
  Pallas kernels: 95.9 us -> 92 us
    pallas_call x1, Pallas kernels: 95.9 us -> 92 us  [shards(): pl.pallas_call(whole_kernel, out_shape=jax.ShapeDtypeStruct((2 * ROWS, 2...]
where the time goes in v6:
time: 94.3 us; the launch traced here: 94.2 us
  Pallas kernels  92 us (98%)
  local copies, waits for them, and re-layouts  2.18 us (2%)
    pallas_call x1, Pallas kernels, shards(): pl.pallas_call(whole_kernel, out_shape=jax.ShapeDtypeStruct((2 * ROWS, 2...  92 us
    reshape x1, local copies, waits for them, and re-layouts, shards(): return decoded.reshape(2 * ROWS, 1, 2 * COLS, OUT)  2.18 us

profile of v6, /device:TPU:66, one launch (start us, length us, event | category | flops | bytes accessed | tf_op | source)
XLA Modules:
  0.0 94.2 jit_solution(6105613972249812251)
XLA Ops:
  0.0 92.0 %decoder_window.1 = bf16[8,208,192]{2,1,0:T(8,128)(2,1)} custom-call(s32[128]{0:T(128)} %videos.1, s32[4]{0:T(128)} %cols.1, bf16[416,384]{1,0:T(8,128)(2,1)} %bitcast.9, f32[384]{0:T(512)} %first_gain.1, f32[384]{0:T(512)} %first_shift.1, bf16[9,1152,384]{2,1,0:T(8,128)(2,1)} %bitcast.6, f32[384]{0:T(512)} %conv_bias.1, f32[384]{0:T(512)} %second_gain.1, ...), custom_call_target="tpu_custom_call" | custom-call | tf_op jit(solution)/shard_map/decoder_window/pallas_call | solution.py:793
  92.0 2.2 %copy.16 = bf16[8,1,208,192]{2,3,1,0:T(8,128)(2,1)} copy(bf16[8,1,208,192]{3,2,0,1:T(8,128)(2,1)} %bitcast.7) | data formatting | bytes 1277952 | tf_op jit(solution)/shard_map/reshape | solution.py:864

commit v7 on v6

--- a/solution.py
+++ b/solution.py
@@ -481,11 +481,12 @@
     kv_across[0].start()
     to_ahead[0][0].start()
     to_behind[0][1].start()
+    q_copies[1].start()
     kv_across[1].start()
     to_ahead[0][1].start()
     to_behind[0][0].start()
-    for copy in q_copies:
-        copy.start()
+    q_copies[2].start()
+    q_copies[0].start()
     kv_across[0].wait_recv()
     to_ahead[1][0].start()
     kv_across[1].wait_recv()

time: 94.3 us -> 94.3 us (level)
  no operation moved by 1% of the time
where the time goes in v7:
time: 94.3 us; the launch traced here: 94.2 us
  Pallas kernels  92 us (98%)
  local copies, waits for them, and re-layouts  2.18 us (2%)
    pallas_call x1, Pallas kernels, shards(): pl.pallas_call(whole_kernel, out_shape=jax.ShapeDtypeStruct((2 * ROWS, 2...  92 us
    reshape x1, local copies, waits for them, and re-layouts, shards(): return decoded.reshape(2 * ROWS, 1, 2 * COLS, OUT)  2.18 us

profile of v7, /device:TPU:66, one launch (start us, length us, event | category | flops | bytes accessed | tf_op | source)
XLA Modules:
  0.0 94.2 jit_solution(17640363758419944754)
XLA Ops:
  0.0 92.0 %decoder_window.1 = bf16[8,208,192]{2,1,0:T(8,128)(2,1)} custom-call(s32[128]{0:T(128)} %videos.1, s32[4]{0:T(128)} %cols.1, bf16[416,384]{1,0:T(8,128)(2,1)} %bitcast.9, f32[384]{0:T(512)} %first_gain.1, f32[384]{0:T(512)} %first_shift.1, bf16[9,1152,384]{2,1,0:T(8,128)(2,1)} %bitcast.6, f32[384]{0:T(512)} %conv_bias.1, f32[384]{0:T(512)} %second_gain.1, ...), custom_call_target="tpu_custom_call" | custom-call | tf_op jit(solution)/shard_map/decoder_window/pallas_call | solution.py:794
  92.0 2.2 %copy.16 = bf16[8,1,208,192]{2,3,1,0:T(8,128)(2,1)} copy(bf16[8,1,208,192]{3,2,0,1:T(8,128)(2,1)} %bitcast.7) | data formatting | bytes 1277952 | tf_op jit(solution)/shard_map/reshape | solution.py:865
